TPU v7x, 512 devices: a whole 4x8x8 slice. The times are simulated.
512 devices in a mesh: lon: 128 (over z_hi, x, y, core), lev: 4 (over z_lo).
Axes of the slice: x: 4, y: 8, z: 8 (z_hi: 2, z_lo: 4; z = z_hi * 4 + z_lo), core: 2. Of those that a mesh axis runs over, the one named last changes fastest.
Arguments:
- latents: bfloat16 [2, 24, 3072, 512], P(None, 'lev', 'lon'), may hold values from -120 to 120
- shift_offset: int32 [1], replicated, may hold values from 1 to 11
- qkv_weight: bfloat16 [512, 1536], replicated, may hold values from -0.25 to 0.25
- proj_weight: bfloat16 [512, 512], replicated, may hold values from -0.25 to 0.25
- post_gain: float32 [512], replicated, may hold values from 0.5 to 1.5
- bias_first_weight: float32 [3, 512], replicated, may hold values from -6 to 6
- bias_first_offset: float32 [512], replicated, may hold values from -3 to 3
- bias_second_weight: float32 [512, 16], replicated, may hold values from -0.25 to 0.25
- dec_gain: float32 [512], replicated, may hold values from 0.5 to 1.5
- kv_weight: bfloat16 [512, 1024], replicated, may hold values from -0.25 to 0.25
- head_weight: bfloat16 [512, 80], replicated, may hold values from -0.25 to 0.25
- level_queries: float32 [8, 512], replicated, may hold values from -120 to 120
- level_order: int32 [8], replicated, may hold values from 0 to 7, each once
Outputs:
- hidden_state_out: bfloat16 [2, 24, 3072, 512], P(None, 'lev', 'lon')
- predicted_tiles: bfloat16 [8, 24, 245760], P('lev', None, 'lon')
Inputs may be any that keep to these rules, and one draw needn't show every extreme that they name: `level_order`: each of 0 to 7 exactly once.
All inputs are finite; a program needn't handle non-finite values.
Results may differ from a plain program's by a relative error of at most 0.017.
Values may be sent and summed in bfloat16 or wider, within the bound.
A program may use at most 128 MiB of HBM per device.

v0:
```python
import math

import jax
import jax.numpy as jnp
from jax import lax
from jax.sharding import PartitionSpec as P

epsilon = 1e-05


def from_behind(value, axis, steps):
    count = lax.axis_size(axis)
    pairs = [(source, (source + steps) % count) for source in range(count)]
    return lax.ppermute(value, axis, pairs)


def bias_table(bias_first_weight, bias_first_offset, bias_second_weight):
    depth_off = (jnp.arange(3, dtype=jnp.float32) - 1.0) * 8.0
    row_off = (jnp.arange(11, dtype=jnp.float32) - 5.0) * 8.0 / 5.0
    col_off = (jnp.arange(23, dtype=jnp.float32) - 11.0) * 8.0 / 11.0
    grid_depth, grid_row, grid_col = jnp.meshgrid(depth_off, row_off, col_off, indexing="ij")
    coords = jnp.stack([grid_depth, grid_row, grid_col], axis=-1).reshape(-1, 3)
    coords = jnp.sign(coords) * jnp.log2(jnp.abs(coords) + 1.0) / 3.0
    hidden = jax.nn.relu(
        jnp.dot(coords, bias_first_weight, precision=lax.Precision.HIGHEST) + bias_first_offset
    )
    table = 16.0 * jax.nn.sigmoid(
        jnp.dot(hidden, bias_second_weight, precision=lax.Precision.HIGHEST)
    )
    head_count = table.shape[1]
    lattice = table.reshape(3, 11, 23, head_count)
    col_part = jnp.stack(
        [lattice[:, :, start : start + 12][:, :, ::-1] for start in range(12)], axis=2
    )
    row_part = jnp.stack([col_part[:, start : start + 6][:, ::-1] for start in range(6)], axis=1)
    depth_part = jnp.stack([row_part[start : start + 2][::-1] for start in range(2)], axis=0)
    arranged = depth_part.transpose(6, 0, 2, 4, 1, 3, 5)
    return arranged.reshape(head_count, 144, 144)


def layer_norm(values):
    centre = values - jnp.mean(values, axis=-1, keepdims=True)
    spread = jnp.mean(centre * centre, axis=-1, keepdims=True)
    return centre * lax.rsqrt(spread + epsilon)


def window_block(strip, position_bias, qkv_weight, proj_weight, post_gain):
    depth_count, row_count, col_count, width_all = strip.shape
    head_count = position_bias.shape[0]
    head_dim = width_all // head_count
    windows = strip.reshape(depth_count // 2, 2, row_count // 6, 6, col_count // 12, 12, width_all)
    windows = windows.transpose(0, 2, 4, 1, 3, 5, 6).reshape(-1, 144, width_all)
    window_count = windows.shape[0]
    packed = jnp.einsum(
        "wtc,cf->wtf", windows, qkv_weight, preferred_element_type=jnp.float32
    ).astype(jnp.bfloat16)
    packed = packed.reshape(window_count, 144, 3, head_count, head_dim)
    scores = jnp.einsum(
        "wqhd,wkhd->whqk", packed[:, :, 0], packed[:, :, 1], preferred_element_type=jnp.float32
    )
    scores = scores / math.sqrt(head_dim) + position_bias[None]
    largest = jnp.max(scores, axis=-1, keepdims=True)
    raised = jnp.exp(scores - largest)
    probabilities = (raised / jnp.sum(raised, axis=-1, keepdims=True)).astype(jnp.bfloat16)
    attended = jnp.einsum(
        "whqk,wkhd->wqhd", probabilities, packed[:, :, 2], preferred_element_type=jnp.float32
    )
    attended = attended.astype(jnp.bfloat16).reshape(window_count, 144, width_all)
    projected = jnp.einsum("wtc,cf->wtf", attended, proj_weight, preferred_element_type=jnp.float32)
    blended = (windows.astype(jnp.float32) + post_gain * layer_norm(projected)).astype(jnp.bfloat16)
    blended = blended.reshape(
        depth_count // 2, row_count // 6, col_count // 12, 2, 6, 12, width_all
    )
    return blended.transpose(0, 3, 1, 4, 2, 5, 6).reshape(
        depth_count, row_count, col_count, width_all
    )


def decode(strip, ordered, dec_gain, kv_weight, head_weight, head_count):
    depth_count, row_count, col_count, width_all = strip.shape
    head_dim = width_all // head_count
    normed = (dec_gain * layer_norm(strip.astype(jnp.float32))).astype(jnp.bfloat16)
    memory = jnp.einsum(
        "zrcd,df->zrcf", normed, kv_weight, preferred_element_type=jnp.float32
    ).astype(jnp.bfloat16)
    key_part = memory[..., :width_all].reshape(
        depth_count, row_count, col_count, head_count, head_dim
    )
    value_part = (
        memory[..., width_all:]
        .reshape(depth_count, row_count, col_count, head_count, head_dim)
        .astype(jnp.float32)
    )

    def one_level(level_query):
        query_part = level_query.astype(jnp.bfloat16).reshape(head_count, head_dim)
        scores = jnp.einsum(
            "hd,zrchd->zrch", query_part, key_part, preferred_element_type=jnp.float32
        ) / math.sqrt(head_dim)
        largest = jnp.max(scores, axis=0, keepdims=True)
        raised = jnp.exp(scores - largest)
        weights = raised / jnp.sum(raised, axis=0, keepdims=True)
        decoded = (
            jnp.sum(weights[..., None] * value_part, axis=0)
            .reshape(row_count, col_count, width_all)
            .astype(jnp.bfloat16)
        )
        result = jnp.einsum(
            "rcd,dp->rcp", decoded, head_weight, preferred_element_type=jnp.float32
        ).astype(jnp.bfloat16)
        return result.reshape(row_count, col_count * head_weight.shape[1])

    return lax.map(one_level, ordered)


def body(
    latents,
    shift_offset,
    qkv_weight,
    proj_weight,
    post_gain,
    bias_first_weight,
    bias_first_offset,
    bias_second_weight,
    dec_gain,
    kv_weight,
    head_weight,
    level_queries,
    level_order,
):
    offset_cols = shift_offset[0]
    col_count = latents.shape[2]
    position_bias = bias_table(bias_first_weight, bias_first_offset, bias_second_weight)
    leading = latents[:, :, :12]
    arrived = from_behind(leading, "lon", -1)
    extended = jnp.concatenate([latents, arrived], axis=2)
    window = lax.dynamic_slice_in_dim(extended, offset_cols, col_count, 2)
    blended = window_block(window, position_bias, qkv_weight, proj_weight, post_gain)
    holder = lax.dynamic_update_slice_in_dim(
        jnp.zeros(extended.shape, jnp.bfloat16), blended, offset_cols, 2
    )
    returned = from_behind(holder[:, :, col_count:], "lon", 1)
    hidden_state_out = jnp.concatenate(
        [holder[:, :, :12] + returned, holder[:, :, 12:col_count]], axis=2
    )
    level_total = level_queries.shape[0]
    selector = (level_order[:, None] == jnp.arange(level_total, dtype=jnp.int32)[None, :]).astype(
        jnp.float32
    )
    ordered = jnp.dot(selector, level_queries, precision=lax.Precision.HIGHEST)
    head_count = bias_second_weight.shape[1]
    isobar_indices = decode(hidden_state_out, ordered, dec_gain, kv_weight, head_weight, head_count)
    predicted_tiles = lax.all_to_all(isobar_indices, "lev", split_axis=0, concat_axis=1, tiled=True)
    return (hidden_state_out, predicted_tiles)


def solution(mesh):
    return jax.shard_map(
        body,
        mesh=mesh,
        in_specs=(
            P(None, "lev", "lon", None),
            P(),
            P(),
            P(),
            P(),
            P(),
            P(),
            P(),
            P(),
            P(),
            P(),
            P(),
            P(),
        ),
        out_specs=(P(None, "lev", "lon", None), P("lev", None, "lon")),
        check_vma=False,
    )
```

profile of v0, /device:TPU:64, one launch (start us, length us, event | category | flops | bytes accessed | tf_op | source)
XLA Modules:
  0.0 268.1 jit_solution(17274475931540662191)
XLA Ops:
  2.4 14.5 %collective-permute-start = (bf16[2,6,12,512]{3,2,1,0:T(8,128)(2,1)}, bf16[2,6,12,512]{3,2,1,0:T(8,128)(2,1)}, u32[]{:S(2)}, u32[]{:S(2)}) collective-permute-start(bf16[2,6,12,512]{3,2,1,0:T(8,128)(2,1)} %slice.87), channel_id=1, source_target_pairs={{0,508},{4,0},{8,4},{12,8},{16,12},{20,16},{24,20},{28,24},{32,28}... | collective-permute-start | bytes 442376 | tf_op jit(solution)/shard_map/ppermute | solution.py:14
  19.4 2.2 fusion.28
  21.9 2.8 %fusion.61 = (f32[3,11,12,16]{2,1,0,3:T(8,128)S(1)}, f32[3,11,12,16]{2,1,0,3:T(8,128)S(1)}, f32[3,11,12,16]{2,1,0,3:T(8,128)S(1)}, f32[3,11,12,16]{2,1,0,3:T(8,1...) fusion(f32[3,11,23,16]{2,1,0,3:T(8,128)S(1)} %reshape.83), kind=kLoop, calls=%fused_computation.104 | loop fusion | bytes 608256 | tf_op jit(solution)/shard_map/slice | solution.py:33
  56.9 12.1 %fusion.60 = (f32[3,6,12,12,16]{3,1,0,4,2:T(8,128)}, f32[3,6,12,12,16]{3,1,0,4,2:T(8,128)}, f32[3,6,12,12,16]{3,1,0,4,2:T(8,128)}, f32[3,6,12,12,16]{3,1,0,4,2:T...) fusion(f32[3,11,12,12,16]{3,1,0,4,2:T(8,128)} %bitcast_dynamic-update-slice_fusion.6), kind=kLoop, calls=%fused_computation.103 | loop fusion | bytes 1990656 | tf_op jit(solution)/shard_map/slice | solution.py:35
  69.0 5.3 %rev.72 = f32[3,6,12,12,16]{3,1,0,4,2:T(8,128)} reverse(f32[3,6,12,12,16]{3,1,0,4,2:T(8,128)} %get-tuple-element.58), dimensions={1} | reverse | bytes 331776 | tf_op jit(solution)/shard_map/rev | solution.py:35
  74.3 3.2 %bitcast_dynamic-update-slice_fusion.5 = f32[3,6,6,12,12,16]{4,2,0,5,3,1:T(8,128)} fusion(f32[3,6,12,12,16]{3,1,0,4,2:T(8,128)} %rev.72), kind=kLoop, calls=%fused_computation.27 | loop fusion | bytes 2525184
  77.5 5.3 %rev.73 = f32[3,6,12,12,16]{3,1,0,4,2:T(8,128)} reverse(f32[3,6,12,12,16]{3,1,0,4,2:T(8,128)} %get-tuple-element.57), dimensions={1} | reverse | bytes 331776 | tf_op jit(solution)/shard_map/rev | solution.py:35
  82.9 5.3 %rev.74 = f32[3,6,12,12,16]{3,1,0,4,2:T(8,128)} reverse(f32[3,6,12,12,16]{3,1,0,4,2:T(8,128)} %get-tuple-element.56), dimensions={1} | reverse | bytes 331776 | tf_op jit(solution)/shard_map/rev | solution.py:35
  88.2 5.3 %rev.75 = f32[3,6,12,12,16]{3,1,0,4,2:T(8,128)} reverse(f32[3,6,12,12,16]{3,1,0,4,2:T(8,128)} %get-tuple-element.55), dimensions={1} | reverse | bytes 331776 | tf_op jit(solution)/shard_map/rev | solution.py:35
  93.5 5.3 %rev.76 = f32[3,6,12,12,16]{3,1,0,4,2:T(8,128)} reverse(f32[3,6,12,12,16]{3,1,0,4,2:T(8,128)} %get-tuple-element.54), dimensions={1} | reverse | bytes 331776 | tf_op jit(solution)/shard_map/rev | solution.py:35
  98.8 5.4 %rev.77 = f32[3,6,12,12,16]{3,1,0,4,2:T(8,128)} reverse(f32[3,6,12,12,16]{3,1,0,4,2:T(8,128)} %get-tuple-element.53), dimensions={1} | reverse | bytes 331776 | tf_op jit(solution)/shard_map/rev | solution.py:35
  104.1 3.4 %bitcast_dynamic-update-slice_fusion.4 = f32[3,6,6,12,12,16]{4,2,0,5,3,1:T(8,128)} fusion(f32[3,6,6,12,12,16]{4,2,0,5,3,1:T(8,128)} %bitcast_dynamic-update-slice_fusion.5, f32[3,6,12,12,16]{3,1,0,4,2:T(8,128)} %rev.73), kind=kLoop, calls=%fused_computation.26 | loop fusion | bytes 4718592
  114.0 11.1 %fusion.59 = (f32[2,6,6,12,12,16]{4,2,0,5,3,1:T(8,128)S(1)}, f32[2,6,6,12,12,16]{4,2,0,5,3,1:T(8,128)}) fusion(f32[3,6,6,12,12,16]{4,2,0,5,3,1:T(8,128)} %bitcast_dynamic-update-slice_fusion), kind=kLoop, calls=%fused_computation.102 | loop fusion | bytes 2654208 | tf_op jit(solution)/shard_map/slice | solution.py:36
  125.1 9.9 %reverse_bitcast_fusion = (f32[1,2,6,6,12,12,16]{5,3,1,6,4,2,0:T(8,128)}, f32[1,2,6,6,12,12,16]{5,3,1,6,4,2,0:T(8,128)}) fusion(f32[2,6,6,12,12,16]{4,2,0,5,3,1:T(8,128)} %get-tuple-element.52, f32[2,6,6,12,12,16]{4,2,0,5,3,1:T(8,128)S(1)} %get-tuple-element.51), kind=kLoop, calls=%fused_computation.15 | loop fusion | bytes 2654208 | tf_op jit(solution)/shard_map/stack | solution.py:36
  135.1 13.7 %maximum_bitcast_fusion = f32[16,2,6,12,2,6,12]{6,5,4,0,3,2,1:T(8,128)} fusion(f32[1,2,6,6,12,12,16]{5,3,1,6,4,2,0:T(8,128)} %get-tuple-element.79, f32[1,2,6,6,12,12,16]{5,3,1,6,4,2,0:T(8,128)} %get-tuple-element.80), kind=kLoop, calls=%fused_computation.14 | loop fusion | flops 331776 | bytes 2654208 | tf_op jit(solution)/shard_map/transpose | solution.py:37
  148.8 13.4 %reshape.100 = f32[16,144,144]{2,0,1:T(8,128)} reshape(f32[16,2,6,12,2,6,12]{6,5,4,0,3,2,1:T(8,128)} %maximum_bitcast_fusion) | data formatting | bytes 2654208 | tf_op jit(solution)/shard_map/add | solution.py:61
  162.2 3.5 %copy.32 = f32[16,144,144]{1,2,0:T(8,128)} copy(f32[16,144,144]{2,0,1:T(8,128)} %reshape.100) | data formatting | bytes 2654208 | tf_op jit(solution)/shard_map/add | solution.py:61
  172.9 2.5 fusion.62
  181.6 13.0 %collective-permute-done.1 = bf16[2,6,12,512]{3,2,1,0:T(8,128)(2,1)S(1)} collective-permute-done((bf16[2,6,12,512]{3,2,1,0:T(8,128)(2,1)S(1)}, bf16[2,6,12,512]{3,2,1,0:T(8,128)(2,1)S(1)}, u32[]{:S(2)}, u32[]{:S(2)}) %collective-permute-start.1) | collective-permute-done | bytes 147488 | tf_op jit(solution)/shard_map/ppermute | solution.py:14
  200.1 55.3 %while.10 = (s32[]{:T(128)}, bf16[8,6,1920]{2,1,0:T(8,128)(2,1)}, bf16[8,512]{1,0:T(8,128)(2,1)S(1)}, bf16[2,6,24,16,32]{4,3,2,1,0:T(8,128)(2,1)S(1)}, f32[2,6,2...) while((s32[]{:T(128)}, bf16[8,6,1920]{2,1,0:T(8,128)(2,1)}, bf16[8,512]{1,0:T(8,128)(2,1)S(1)}, ...), condition=%wide.region_10.11_spmd, body=%wide.region_6.10_spmd.sunk | while | flops 12356354 | bytes 1878609 | solution.py:113
  202.6 2.2 multiply_reduce_fusion.3
  216.4 2.2 multiply_reduce_fusion.3
  223.3 2.2 multiply_reduce_fusion.3
  255.4 11.8 %all_to_all.18 = bf16[8,6,1920]{2,1,0:T(8,128)(2,1)S(1)} all-to-all(bf16[8,6,1920]{2,1,0:T(8,128)(2,1)} %get-tuple-element.34), channel_id=1, replica_groups=mesh['lon'=128,'lev'=4] {'lev'}, dimensions={0} | all-to-all | bytes 368640 | tf_op jit(solution)/shard_map/all_to_all | solution.py:153
  (197 shorter events, 110.1 us)
Async XLA Ops:
  0.6 167.5 %copy-start = (bf16[512,1536]{1,0:T(8,128)(2,1)S(1)}, bf16[512,1536]{1,0:T(8,128)(2,1)}, u32[]{:S(2)}) copy-start(bf16[512,1536]{1,0:T(8,128)(2,1)} %param.17) | copy-start | bytes 4718596
  2.4 164.0 %collective-permute-start = (bf16[2,6,12,512]{3,2,1,0:T(8,128)(2,1)}, bf16[2,6,12,512]{3,2,1,0:T(8,128)(2,1)}, u32[]{:S(2)}, u32[]{:S(2)}) collective-permute-start(bf16[2,6,12,512]{3,2,1,0:T(8,128)(2,1)} %slice.87), channel_id=1, source_target_pairs={{0,508},{4,0},{8,4},{12,8},{16,12},{20,16},{24,20},{28,24},{32,28}... | collective-permute-start | bytes 442376 | tf_op jit(solution)/shard_map/ppermute | solution.py:14
  24.7 15.3 %copy-start.6 = (f32[3,11,12,16]{2,1,0,3:T(8,128)S(1)}, f32[3,11,12,16]{2,1,0,3:T(8,128)}, u32[]{:S(2)}) copy-start(f32[3,11,12,16]{2,1,0,3:T(8,128)} %get-tuple-element.67) | copy-start | bytes 76036
  41.9 11.8 %copy-start.7 = (f32[3,11,12,16]{2,1,0,3:T(8,128)S(1)}, f32[3,11,12,16]{2,1,0,3:T(8,128)}, u32[]{:S(2)}) copy-start(f32[3,11,12,16]{2,1,0,3:T(8,128)} %rev.68) | copy-start | bytes 76036
  42.3 10.7 %copy-start.8 = (f32[3,11,12,16]{2,1,0,3:T(8,128)S(1)}, f32[3,11,12,16]{2,1,0,3:T(8,128)}, u32[]{:S(2)}) copy-start(f32[3,11,12,16]{2,1,0,3:T(8,128)} %rev.67) | copy-start | bytes 76036
  104.1 3.4 %copy-start.4 = (f32[3,6,12,12,16]{3,1,0,4,2:T(8,128)S(1)}, f32[3,6,12,12,16]{3,1,0,4,2:T(8,128)}, u32[]{:S(2)}) copy-start(f32[3,6,12,12,16]{3,1,0,4,2:T(8,128)} %rev.74) | copy-start | bytes 497668
  104.1 5.0 %copy-start.3 = (f32[3,6,12,12,16]{3,1,0,4,2:T(8,128)S(1)}, f32[3,6,12,12,16]{3,1,0,4,2:T(8,128)}, u32[]{:S(2)}) copy-start(f32[3,6,12,12,16]{3,1,0,4,2:T(8,128)} %rev.75) | copy-start | bytes 497668
  107.5 3.2 %copy-start.1 = (f32[3,6,12,12,16]{3,1,0,4,2:T(8,128)S(1)}, f32[3,6,12,12,16]{3,1,0,4,2:T(8,128)}, u32[]{:S(2)}) copy-start(f32[3,6,12,12,16]{3,1,0,4,2:T(8,128)} %rev.76) | copy-start | bytes 497668
  109.1 3.2 %copy-start.2 = (f32[3,6,12,12,16]{3,1,0,4,2:T(8,128)S(1)}, f32[3,6,12,12,16]{3,1,0,4,2:T(8,128)}, u32[]{:S(2)}) copy-start(f32[3,6,12,12,16]{3,1,0,4,2:T(8,128)} %rev.77) | copy-start | bytes 497668
  162.2 4.2 %copy-start.10 = (bf16[2,6,24,512]{3,2,1,0:T(8,128)(2,1)S(1)}, bf16[2,6,24,512]{3,2,1,0:T(8,128)(2,1)}, u32[]{:S(2)}) copy-start(bf16[2,6,24,512]{3,2,1,0:T(8,128)(2,1)} %param.15) | copy-start | bytes 884740
  171.2 1.7 copy-start.5
  175.4 1.0 copy-start.11
  175.5 1.8 copy-start.12
  175.9 5.5 %copy-start.13 = (f32[8,512]{1,0:T(8,128)S(1)}, f32[8,512]{1,0:T(8,128)}, u32[]{:S(2)}) copy-start(f32[8,512]{1,0:T(8,128)} %param.26) | copy-start | bytes 49156
  175.9 5.5 %copy-start.15 = (s32[8]{0:T(128)S(1)}, s32[8]{0:T(128)}, u32[]{:S(2)}) copy-start(s32[8]{0:T(128)} %param.27) | copy-start | bytes 100
  176.0 19.7 %copy-start.14 = (f32[512]{0:T(512)S(1)}, f32[512]{0:T(512)}, u32[]{:S(2)}) copy-start(f32[512]{0:T(512)} %param.23) | copy-start | bytes 6148
  179.3 15.4 %collective-permute-start.1 = (bf16[2,6,12,512]{3,2,1,0:T(8,128)(2,1)S(1)}, bf16[2,6,12,512]{3,2,1,0:T(8,128)(2,1)S(1)}, u32[]{:S(2)}, u32[]{:S(2)}) collective-permute-start(bf16[2,6,12,512]{3,2,1,0:T(8,128)(2,1)S(1)} %slice.140), channel_id=1, source_target_pairs={{0,4},{4,8},{8,12},{12,16},{16,20},{20,24},{24,28},{28,32},{32,36}... | collective-permute-start | bytes 442376 | tf_op jit(solution)/shard_map/ppermute | solution.py:14
  194.9 0.7 copy-start.9
where the time goes:
time: 271 us; the launch traced here: 268 us
  local copies, waits for them, and re-layouts  153 us (56%)
  other arithmetic  36.9 us (14%)
  matrix products  34.5 us (13%)
  starting transfers between devices  16.7 us (6%)
  waiting for transfers between devices  13 us (5%)
  blocking collectives  11.8 us (4%)
    rev x6, local copies, waits for them, and re-layouts, bias_table(): col_part[:, start:start + 6][:, ::-1]  31.9 us
    unnamed x49, local copies, waits for them, and re-layouts  29.5 us
    reduce_sum x8, other arithmetic, one_level(): jnp.sum(weights[..., None] * value_part, axis=0)  17.6 us
    add x2, local copies, waits for them, and re-layouts, window_block(): scores = scores / math.sqrt(head_dim) + position_bias[None]  16.9 us
    ppermute x2, starting transfers between devices, from_behind(): return lax.ppermute(value, axis, pairs)  16.7 us
    dot_general x8, matrix products, one_level(): jnp.einsum('hd,zrchd->zrch', query_part, key_part, preferred_element_type...  16.3 us
    rev x12, local copies, waits for them, and re-layouts, bias_table(): lattice[:, :, start:start + 12][:, :, ::-1]  15.8 us
    transpose x1, other arithmetic, bias_table(): arranged = depth_part.transpose(6, 0, 2, 4, 1, 3, 5)  13.7 us
  transfers between devices with their start and end apart: 2, of which 1 were waited for; matrix products, arithmetic and copies ran while one was open for 56% of the time, Pallas kernels for 0%

commit v1 on v0

v1 whole, which is shorter than its diff:
```python
import functools
import math

import jax
import jax.numpy as jnp
import numpy as np
from jax import lax
from jax.experimental import pallas as pl
from jax.experimental.pallas import tpu as pltpu
from jax.sharding import PartitionSpec as P

EPSILON = 1e-05
WIDTH = 512
HEADS = 16
HEAD_DIM = WIDTH // HEADS
TOKENS = 144
OWN = 288
TILE = 80
ROW = 24 * TILE
LOG2E = math.log2(math.e)
BF16 = jnp.bfloat16
F32 = jnp.float32


def dot_nn(a, b):
    return lax.dot_general(a, b, (((1,), (0,)), ((), ())), preferred_element_type=F32)


def dot_nt(a, b):
    return lax.dot_general(a, b, (((1,), (1,)), ((), ())), preferred_element_type=F32)


def split(value):
    high = value.astype(BF16)
    return high, (value - high.astype(F32)).astype(BF16)


def coordinate(steps):
    return np.sign(steps) * np.log2(np.abs(steps) + 1.0) / 3.0


def constants():
    place = np.arange(256)
    row, col = place // 23, place % 23
    inside = place < 253
    coords = np.zeros((256, 2), np.float32)
    coords[:, 0] = np.where(inside, coordinate((5 - row) * 8.0 / 5.0), 0.0)
    coords[:, 1] = np.where(inside, coordinate((11 - col) * 8.0 / 11.0), 0.0)
    compact = np.zeros((256, 256), np.float32)
    for part in range(2):
        for k in range(10):
            for x in range(12):
                compact[(k + 1 - part) * 23 + x, part * 128 + 12 * k + x] = 1.0
    index = np.zeros((OWN, 8), np.int32)
    cell = np.arange(OWN)
    block, rest = cell // TOKENS, cell % TOKENS
    index[:, 0] = rest // 12 * 24
    index[:, 1] = block * 12 + rest % 12
    index[:, 2] = cell // 24 * 12
    index[:, 3] = cell % 24
    index[:, 4] = rest % 12
    slot, lat = cell // 24, cell % 24
    index[:48, 5] = (lat // 6 * 16 + slot * 6 + lat % 6)[:48]
    return coords, compact.astype(BF16), index


def norm(values):
    centre = values - jnp.mean(values, axis=-1, keepdims=True)
    spread = jnp.mean(centre * centre, axis=-1, keepdims=True)
    return centre * lax.rsqrt(spread + EPSILON)


def kernel(
    lon_count,
    lev_count,
    offset_ref,
    order_ref,
    latents_hbm,
    wqkv_hbm,
    wproj_hbm,
    wkv_hbm,
    post_gain_ref,
    first_ref,
    first_offset_ref,
    second_ref,
    dec_gain_ref,
    head_ref,
    queries_ref,
    coords_ref,
    compact_ref,
    index_ref,
    hidden_ref,
    tiles_ref,
    own_ref,
    wqkv_ref,
    wproj_ref,
    wkv_ref,
    turned_ref,
    halo_ref,
    shifted_ref,
    lattice_ref,
    packed_ref,
    packed_halo_ref,
    attended_ref,
    level_query_ref,
    result_ref,
    send_ref,
    receive_ref,
    local_sem,
    halo_send_sem,
    halo_receive_sem,
    tile_send_sem,
    tile_receive_sem,
):
    lon = lax.axis_index("lon")
    lev = lax.axis_index("lev")
    west = lax.rem(lon + lon_count - 1, lon_count)
    east = lax.rem(lon + 1, lon_count)
    mesh_id = pl.DeviceIdType.MESH

    barrier = pltpu.get_barrier_semaphore()
    for side in (west, east):
        pl.semaphore_signal(barrier, inc=1, device_id=(side, lev), device_id_type=mesh_id)
    for step in range(1, lev_count):
        pl.semaphore_signal(
            barrier,
            inc=1,
            device_id=(lon, lax.rem(lev + step, lev_count)),
            device_id_type=mesh_id,
        )

    loads = []
    for place, (source, target) in enumerate(
        (
            (latents_hbm, own_ref),
            (wqkv_hbm, wqkv_ref),
            (wproj_hbm, wproj_ref),
            (wkv_hbm, wkv_ref),
        )
    ):
        load = pltpu.make_async_copy(source, target, local_sem.at[place])
        load.start()
        loads.append(load)

    offset = offset_ref[0]

    turned_col = index_ref[:, 1:2] + offset
    turned_col = index_ref[:, 0:1] + jnp.where(turned_col >= 24, turned_col - 24, turned_col)
    cells = lax.broadcasted_iota(jnp.int32, (OWN, OWN), 1)
    turn = jnp.where(cells == turned_col, 1.0, 0.0).astype(BF16)
    loads[0].wait()
    turned_ref[...] = dot_nn(turn, own_ref[...]).astype(BF16)

    pl.semaphore_wait(barrier, 2 + lev_count - 1)
    halo_copies = []
    for place, side in enumerate((east, west)):
        copy = pltpu.make_async_remote_copy(
            src_ref=turned_ref.at[pl.ds(TOKENS, TOKENS)],
            dst_ref=halo_ref.at[place],
            send_sem=halo_send_sem.at[place],
            recv_sem=halo_receive_sem.at[place],
            device_id=(side, lev),
            device_id_type=mesh_id,
        )
        copy.start()
        halo_copies.append(copy)

    second_high, second_low = split(jnp.transpose(second_ref[...]))
    second_both = jnp.concatenate([second_high, second_low], axis=0)
    flat_part = (
        coords_ref[:, 0:1] * first_ref[1:2, :]
        + coords_ref[:, 1:2] * first_ref[2:3, :]
        + first_offset_ref[...]
    )
    for a in range(3):
        depth_coord = float(coordinate(np.float64((1 - a) * 8.0)))
        hidden = jnp.maximum(flat_part + depth_coord * first_ref[0:1, :], 0.0)
        hidden_high, hidden_low = split(hidden)
        both = dot_nt(second_both, hidden_high)
        logits = both[:HEADS] + both[HEADS:] + dot_nt(second_high, hidden_low)
        table = (16.0 * LOG2E) / (1.0 + jnp.exp(-logits))
        for x in range(12):
            rolled = table if x == 11 else pltpu.roll(table, 256 - (11 - x), 1)
            high, low = split(rolled)
            shifted_ref[pl.ds(x * HEADS, HEADS), :] = high
            shifted_ref[pl.ds((12 + x) * HEADS, HEADS), :] = low
        spread_out = dot_nn(shifted_ref[...], compact_ref[...])
        spread_out = spread_out[:192] + spread_out[192:]
        lattice_ref[a, pl.ds(0, 192), :] = spread_out[:, :128]
        lattice_ref[a, pl.ds(192, 192), :] = spread_out[:, 128:]

    loads[1].wait()
    turned = turned_ref[...]
    scale = LOG2E / math.sqrt(HEAD_DIM)
    packed_ref[:, :WIDTH] = (dot_nn(turned, wqkv_ref[:, :WIDTH]) * scale).astype(BF16)
    packed_ref[:, WIDTH:] = dot_nn(turned, wqkv_ref[:, WIDTH:]).astype(BF16)

    for copy in halo_copies:
        copy.wait()
    upper = index_ref[:TOKENS, 4:5] >= 12 - offset
    halo = jnp.where(upper, halo_ref[1].astype(F32), halo_ref[0].astype(F32)).astype(BF16)
    packed_halo_ref[...] = dot_nn(halo, wqkv_ref[:, WIDTH:]).astype(BF16)

    lane256 = lax.broadcasted_iota(jnp.int32, (TOKENS, 256), 1)
    lane128 = lax.broadcasted_iota(jnp.int32, (24, 128), 1)
    edge = pl.ds(TOKENS, TOKENS)
    zero = jnp.zeros((), BF16)
    for half in range(2):
        lanes = pl.ds(256 * half, 256)
        q_inner = packed_ref[pl.ds(0, TOKENS), lanes]
        k_inner = packed_ref[pl.ds(0, TOKENS), pl.ds(WIDTH + 256 * half, 256)]
        v_inner = packed_ref[pl.ds(0, TOKENS), pl.ds(2 * WIDTH + 256 * half, 256)]
        q_edge = packed_ref[edge, lanes]
        k_edge = packed_ref[edge, pl.ds(WIDTH + 256 * half, 256)].astype(F32)
        v_edge = packed_ref[edge, pl.ds(2 * WIDTH + 256 * half, 256)].astype(F32)
        k_halo = packed_halo_ref[:, lanes].astype(F32)
        v_halo = packed_halo_ref[:, pl.ds(WIDTH + 256 * half, 256)].astype(F32)
        k_upper = jnp.where(upper, k_edge, k_halo).astype(BF16)
        k_lower = jnp.where(upper, k_halo, k_edge).astype(BF16)
        v_upper = jnp.where(upper, v_edge, v_halo).astype(BF16)
        v_lower = jnp.where(upper, v_halo, v_edge).astype(BF16)
        q_upper = jnp.where(upper, q_edge.astype(F32), 0.0).astype(BF16)
        q_lower = jnp.where(upper, 0.0, q_edge.astype(F32)).astype(BF16)
        out_inner = jnp.zeros((TOKENS, 256), F32)
        out_upper = jnp.zeros((TOKENS, 256), F32)
        out_lower = jnp.zeros((TOKENS, 256), F32)
        for local_head in range(8):
            h = 8 * half + local_head
            mine = lane256 // HEAD_DIM == local_head
            lattice = [lattice_ref[a, pl.ds(h, 24, stride=HEADS), :] for a in range(3)]
            pieces = []
            for dz in range(2):
                for m in range(3):
                    start = (4 - 2 * m) * 12
                    near = lattice[1 - dz]
                    if start:
                        near = pltpu.roll(near, 128 - start, 1)
                    far = pltpu.roll(lattice[2 - dz], 72 - start, 1)
                    pieces.append(
                        jnp.concatenate([jnp.where(lane128 < 72, near, far), far[:, :16]], axis=1)
                    )
            bias = jnp.concatenate(pieces, axis=0)

            def soft(scores):
                raised = jnp.exp2(scores - jnp.max(scores, axis=-1, keepdims=True))
                total = jnp.sum(raised, axis=-1, keepdims=True)
                return (raised * (1.0 / total)).astype(BF16)

            weights = soft(dot_nt(jnp.where(mine, q_inner, zero), k_inner) + bias)
            out_inner = jnp.where(mine, dot_nn(weights, v_inner), out_inner)
            weights = soft(
                dot_nt(jnp.where(mine, q_upper, zero), k_upper)
                + dot_nt(jnp.where(mine, q_lower, zero), k_lower)
                + bias
            )
            out_upper = jnp.where(mine, dot_nn(weights, v_upper), out_upper)
            out_lower = jnp.where(mine, dot_nn(weights, v_lower), out_lower)
        attended_ref[pl.ds(0, TOKENS), lanes] = out_inner.astype(BF16)
        attended_ref[edge, lanes] = jnp.where(upper, out_upper, out_lower).astype(BF16)

    loads[2].wait()
    projected = dot_nn(attended_ref[...], wproj_ref[...])
    mixed = (turned_ref[...].astype(F32) + post_gain_ref[...] * norm(projected)).astype(BF16)
    back_col = index_ref[:, 3:4] - offset
    back_col = jnp.where(back_col < 0, back_col + 24, back_col)
    back_col = index_ref[:, 2:3] + jnp.where(back_col >= 12, back_col + (TOKENS - 12), back_col)
    turn_back = jnp.where(cells == back_col, 1.0, 0.0).astype(BF16)
    state = dot_nn(turn_back, mixed)
    hidden_ref[...] = state.astype(BF16)

    normed = (dec_gain_ref[...] * norm(state)).astype(BF16)
    loads[3].wait()
    keys = dot_nn(normed, wkv_ref[:, :WIDTH]).astype(BF16)
    values = dot_nn(normed, wkv_ref[:, WIDTH:]).astype(BF16).astype(F32)
    head_lane = lax.broadcasted_iota(jnp.int32, (HEADS, WIDTH), 1) // HEAD_DIM
    head_row = lax.broadcasted_iota(jnp.int32, (HEADS, WIDTH), 0)
    for i in range(8):
        query = queries_ref[pl.ds(order_ref[i], 1), :]
        level_query_ref[pl.ds(i * HEADS, HEADS), :] = jnp.where(
            head_lane == head_row, query, 0.0
        ).astype(BF16)
    scores = dot_nt(keys, level_query_ref[...]) * (0.5 / math.sqrt(HEAD_DIM))
    upper_weight = 0.5 + 0.5 * jnp.tanh(scores[:TOKENS] - scores[TOKENS:])
    weight_high, weight_low = split(upper_weight)
    weight_both = jnp.concatenate([weight_high, weight_low], axis=1)
    expand = jnp.where(
        lax.broadcasted_iota(jnp.int32, (256, WIDTH), 0) % HEADS
        == lax.broadcasted_iota(jnp.int32, (256, WIDTH), 1) // HEAD_DIM,
        1.0,
        0.0,
    ).astype(BF16)
    level_lane = lane256 % 128 // HEADS
    value_lower = values[TOKENS:]
    value_step = values[:TOKENS] - value_lower
    result_ref[pl.ds(8 * TOKENS, 96), :] = jnp.zeros((96, 128), F32)
    for i in range(8):
        wide = dot_nn(jnp.where(level_lane == i, weight_both, zero), expand)
        decoded = (value_lower + wide * value_step).astype(BF16)
        result_ref[pl.ds(i * TOKENS, TOKENS), :TILE] = dot_nn(decoded, head_ref[...])
    lane16 = lax.broadcasted_iota(jnp.int32, (16, 128), 1)
    for target in range(lev_count):
        turned_tiles = []
        for x in range(24):
            slab = result_ref[pl.ds(target * 2 * TOKENS + x, 16, stride=24), :]
            turned_tiles.append(pltpu.roll(slab, x * TILE % 128, 1) if x * TILE % 128 else slab)
        for k in range(ROW // 128):
            first = 128 * k // TILE
            tile = turned_tiles[first]
            for x in range(first + 1, (128 * k + 127) // TILE + 1):
                tile = jnp.where(lane16 >= TILE * x - 128 * k, turned_tiles[x], tile)
            send_ref[target, :, pl.ds(128 * k, 128)] = tile.astype(BF16)

    tile_copies = []
    for step in range(1, lev_count):
        target = lax.rem(lev + step, lev_count)
        copy = pltpu.make_async_remote_copy(
            src_ref=send_ref.at[target],
            dst_ref=receive_ref.at[lev],
            send_sem=tile_send_sem.at[step - 1],
            recv_sem=tile_receive_sem.at[step - 1],
            device_id=(lon, target),
            device_id_type=mesh_id,
        )
        copy.start()
        tile_copies.append(copy)
    receive_ref[pl.ds(lev, 1)] = send_ref[pl.ds(lev, 1)]
    for copy in tile_copies:
        copy.wait()
    gather = jnp.where(
        lax.broadcasted_iota(jnp.int32, (48, 16 * lev_count), 1) == index_ref[:48, 5:6], 1.0, 0.0
    ).astype(BF16)
    received = receive_ref[...].reshape(16 * lev_count, ROW)
    tiles_ref[...] = dot_nn(gather, received).astype(BF16)


def body(
    latents,
    shift_offset,
    qkv_weight,
    proj_weight,
    post_gain,
    bias_first_weight,
    bias_first_offset,
    bias_second_weight,
    dec_gain,
    kv_weight,
    head_weight,
    level_queries,
    level_order,
):
    lon_count = lax.axis_size("lon")
    lev_count = lax.axis_size("lev")
    coords, compact, index = constants()
    smem = pl.BlockSpec(memory_space=pltpu.SMEM)
    vmem = pl.BlockSpec(memory_space=pltpu.VMEM)
    anywhere = pl.BlockSpec(memory_space=pl.ANY)
    dma = pltpu.SemaphoreType.DMA
    hidden, tiles = pl.pallas_call(
        functools.partial(kernel, lon_count, lev_count),
        out_shape=(
            jax.ShapeDtypeStruct((OWN, WIDTH), BF16),
            jax.ShapeDtypeStruct((48, ROW), BF16),
        ),
        in_specs=[smem, smem] + [anywhere] * 4 + [vmem] * 10,
        out_specs=(vmem, vmem),
        scratch_shapes=[
            pltpu.VMEM((OWN, WIDTH), BF16),
            pltpu.VMEM((WIDTH, 3 * WIDTH), BF16),
            pltpu.VMEM((WIDTH, WIDTH), BF16),
            pltpu.VMEM((WIDTH, 2 * WIDTH), BF16),
            pltpu.VMEM((OWN, WIDTH), BF16),
            pltpu.VMEM((2, TOKENS, WIDTH), BF16),
            pltpu.VMEM((384, 256), BF16),
            pltpu.VMEM((3, 384, 128), F32),
            pltpu.VMEM((OWN, 3 * WIDTH), BF16),
            pltpu.VMEM((TOKENS, 2 * WIDTH), BF16),
            pltpu.VMEM((OWN, WIDTH), BF16),
            pltpu.VMEM((128, WIDTH), BF16),
            pltpu.VMEM((8 * TOKENS + 96, 128), F32),
            pltpu.VMEM((lev_count, 16, ROW), BF16),
            pltpu.VMEM((lev_count, 16, ROW), BF16),
            dma((4,)),
            dma((2,)),
            dma((2,)),
            dma((lev_count - 1,)),
            dma((lev_count - 1,)),
        ],
        compiler_params=pltpu.CompilerParams(
            collective_id=0, has_side_effects=True, vmem_limit_bytes=40 * 1024 * 1024
        ),
    )(
        shift_offset,
        level_order,
        latents.reshape(OWN, WIDTH),
        qkv_weight,
        proj_weight,
        kv_weight,
        post_gain.reshape(1, WIDTH),
        bias_first_weight,
        bias_first_offset.reshape(1, WIDTH),
        bias_second_weight,
        dec_gain.reshape(1, WIDTH),
        head_weight,
        level_queries,
        jnp.asarray(coords),
        jnp.asarray(compact),
        jnp.asarray(index),
    )
    return hidden.reshape(latents.shape), tiles.reshape(2, 24, ROW)


def solution(mesh):
    return jax.shard_map(
        body,
        mesh=mesh,
        in_specs=(P(None, "lev", "lon", None),) + (P(),) * 12,
        out_specs=(P(None, "lev", "lon", None), P("lev", None, "lon")),
        check_vma=False,
    )
```

time: 271 us -> 50.7 us (0.19)
  local copies, waits for them, and re-layouts: 153 us -> 14.7 us
  other arithmetic: 36.9 us -> 0 us
  matrix products: 34.5 us -> 0 us
  Pallas kernels: 0 us -> 34 us
  starting transfers between devices: 16.7 us -> 0 us
  waiting for transfers between devices: 13 us -> 0 us
  blocking collectives: 11.8 us -> 0 us
    rev x18 -> x0, local copies, waits for them, and re-layouts: 47.7 us -> none  [the longest x6 31.9 us: bias_table(): col_part[:, start:start + 6][:, ::-1]]
    dot_general x24 -> x0, matrix products: 34.5 us -> none  [the longest x8 16.3 us: one_level(): jnp.einsum('hd,zrchd->zrch', query_part, key_part, preferred_element_type...]
    pallas_call x0 -> x1, Pallas kernels: none -> 34 us  [body(): pl.pallas_call(functools.partial(kernel, lon_count, lev_count), out_shape...]
    slice x5 -> x0, local copies, waits for them, and re-layouts: 27.8 us -> none  [the longest x1 12.1 us: bias_table(): col_part[:, start:start + 6][:, ::-1]]
    reduce_sum x19 -> x0, other arithmetic: 18.6 us -> none  [the longest x8 17.6 us: one_level(): jnp.sum(weights[..., None] * value_part, axis=0)]
    add x2 -> x0, local copies, waits for them, and re-layouts: 16.9 us -> none  [window_block(): scores = scores / math.sqrt(head_dim) + position_bias[None]]
    ppermute x2 -> x0, starting transfers between devices: 16.7 us -> none  [from_behind(): return lax.ppermute(value, axis, pairs)]
    unnamed x49 -> x30, local copies, waits for them, and re-layouts: 29.5 us -> 14.7 us
  transfers between devices with their start and end apart: 2 -> 0, of which waited for: 1 -> 0; matrix products, arithmetic and copies ran while one was open for 56% -> 0% of each run, Pallas kernels for 0% -> 0%
where the time goes in v1:
time: 50.7 us; the launch traced here: 50.1 us
  Pallas kernels  34 us (67%)
  local copies, waits for them, and re-layouts  14.7 us (29%)
  between operations  1.32 us (3%)
    pallas_call x1, Pallas kernels, body(): pl.pallas_call(functools.partial(kernel, lon_count, lev_count), out_shape...  34 us
    unnamed x30, local copies, waits for them, and re-layouts  14.7 us

profile of v1, /device:TPU:64, one launch (start us, length us, event | category | flops | bytes accessed | tf_op | source)
XLA Modules:
  0.0 50.1 jit_solution(4856987142136052069)
XLA Ops:
  1.3 1.0 %copy.19.head_ref = bf16[512,80]{1,0:T(8,128)(2,1)S(1)} copy(bf16[512,80]{0,1:T(8,128)(2,1)} %param.26) | data formatting | bytes 163840 | tf_op args[10]
  2.3 0.9 %copy.18.second_ref = f32[512,16]{1,0:T(8,128)S(1)} copy(f32[512,16]{0,1:T(8,128)} %param.23) | data formatting | bytes 65536 | tf_op args[7]
  3.2 0.0 copy-start
  3.2 1.4 %copy-done = bf16[512,1536]{1,0:T(8,128)(2,1)S(1)} copy-done((bf16[512,1536]{1,0:T(8,128)(2,1)S(1)}, bf16[512,1536]{1,0:T(8,128)(2,1)}, u32[]{:S(2)}) %copy-start) | copy-done | bytes 1572888
  4.6 0.0 copy-start.1
  4.6 1.2 %copy-done.1 = bf16[512,1024]{1,0:T(8,128)(2,1)S(1)} copy-done((bf16[512,1024]{1,0:T(8,128)(2,1)S(1)}, bf16[512,1024]{1,0:T(8,128)(2,1)}, u32[]{:S(2)}) %copy-start.1) | copy-done | bytes 1048600
  5.8 0.0 copy-start.2
  5.8 1.0 %copy-done.2 = bf16[512,512]{1,0:T(8,128)(2,1)S(1)} copy-done((bf16[512,512]{1,0:T(8,128)(2,1)S(1)}, bf16[512,512]{1,0:T(8,128)(2,1)}, u32[]{:S(2)}) %copy-start.2) | copy-done | bytes 524312
  6.9 0.0 copy-start.3
  6.9 1.0 %copy-done.3 = bf16[2,6,24,512]{3,2,1,0:T(8,128)(2,1)S(1)} copy-done((bf16[2,6,24,512]{3,2,1,0:T(8,128)(2,1)S(1)}, bf16[2,6,24,512]{3,2,1,0:T(8,128)(2,1)}, u32[]{:S(2)}) %copy-start.3) | copy-done | bytes 294936
  7.8 0.0 copy-start.4
  7.8 0.9 %copy-done.4 = s32[288,8]{1,0:T(8,128)S(1)} copy-done((s32[288,8]{1,0:T(8,128)S(1)}, s32[288,8]{1,0:T(8,128)}, u32[]{:S(2)}) %copy-start.4) | copy-done | bytes 9240
  8.7 0.0 copy-start.5
  8.7 0.9 %copy-done.5 = bf16[256,256]{1,0:T(8,128)(2,1)S(1)} copy-done((bf16[256,256]{1,0:T(8,128)(2,1)S(1)}, bf16[256,256]{1,0:T(8,128)(2,1)}, u32[]{:S(2)}) %copy-start.5) | copy-done | bytes 131096
  9.6 0.9 %copy-done.6 = f32[256,2]{1,0:T(8,128)S(1)} copy-done((f32[256,2]{1,0:T(8,128)S(1)}, f32[256,2]{1,0:T(8,128)}, u32[]{:S(2)}) %copy-start.6) | copy-done | bytes 2072
  10.5 0.7 %copy-done.7 = f32[8,512]{1,0:T(8,128)S(1)} copy-done((f32[8,512]{1,0:T(8,128)S(1)}, f32[8,512]{1,0:T(8,128)}, u32[]{:S(2)}) %copy-start.7) | copy-done | bytes 16408
  11.3 0.7 %copy-done.8 = f32[3,512]{1,0:T(4,128)S(1)} copy-done((f32[3,512]{1,0:T(4,128)S(1)}, f32[3,512]{1,0:T(4,128)}, u32[]{:S(2)}) %copy-start.8) | copy-done | bytes 6168
  12.0 0.7 %copy-done.9 = f32[512]{0:T(512)S(1)} copy-done((f32[512]{0:T(512)S(1)}, f32[512]{0:T(512)}, u32[]{:S(2)}) %copy-start.9) | copy-done | bytes 2072
  12.6 0.7 %copy-done.10 = f32[512]{0:T(512)S(1)} copy-done((f32[512]{0:T(512)S(1)}, f32[512]{0:T(512)}, u32[]{:S(2)}) %copy-start.10) | copy-done | bytes 2072
  13.3 0.7 %copy-done.11 = f32[512]{0:T(512)S(1)} copy-done((f32[512]{0:T(512)S(1)}, f32[512]{0:T(512)}, u32[]{:S(2)}) %copy-start.11) | copy-done | bytes 2072
  14.0 0.7 %copy-done.12 = s32[8]{0:T(128)S(1)} copy-done((s32[8]{0:T(128)S(1)}, s32[8]{0:T(128)}, u32[]{:S(2)}) %copy-start.12) | copy-done | bytes 56
  14.7 34.0 %shard_map.167 = (bf16[288,512]{1,0:T(8,128)(2,1)S(1)}, bf16[48,1920]{1,0:T(8,128)(2,1)S(1)}) custom-call(s32[1]{0:T(128)S(6)} %copy.22.offset_ref, s32[8]{0:T(128)S(1)} %copy-done.12, bf16[288,512]{1,0:T(8,128)(2,1)S(1)} %bitcast.6, bf16[512,1536]{1,0:T(8,128)(2,1)S(1)} %copy-done, bf16[512,512]{1,0:T(8,128)(2,1)S(1)} %copy-done.2, ...), custom_call_target="tpu_custom_call" | custom-call | tf_op jit(solution)/shard_map/pallas_call | solution.py:358
  48.7 0.7 %copy.23 = bf16[2,6,24,512]{3,2,1,0:T(8,128)(2,1)} copy(bf16[2,6,24,512]{3,2,1,0:T(8,128)(2,1)S(1)} %bitcast.7) | data formatting | bytes 589824
  49.4 0.7 %copy.24 = bf16[2,24,1920]{2,1,0:T(8,128)(2,1)} copy(bf16[2,24,1920]{2,1,0:T(8,128)(2,1)S(1)} %bitcast.8) | data formatting | bytes 368640
  (7 shorter events, 0.0 us)
Async XLA Ops:
  3.2 1.4 %copy-start = (bf16[512,1536]{1,0:T(8,128)(2,1)S(1)}, bf16[512,1536]{1,0:T(8,128)(2,1)}, u32[]{:S(2)}) copy-start(bf16[512,1536]{1,0:T(8,128)(2,1)} %wqkv_hbm.1) | copy-start | bytes 4718596
  4.6 1.2 %copy-start.1 = (bf16[512,1024]{1,0:T(8,128)(2,1)S(1)}, bf16[512,1024]{1,0:T(8,128)(2,1)}, u32[]{:S(2)}) copy-start(bf16[512,1024]{1,0:T(8,128)(2,1)} %wkv_hbm.1) | copy-start | bytes 3145732
  5.8 1.0 %copy-start.2 = (bf16[512,512]{1,0:T(8,128)(2,1)S(1)}, bf16[512,512]{1,0:T(8,128)(2,1)}, u32[]{:S(2)}) copy-start(bf16[512,512]{1,0:T(8,128)(2,1)} %wproj_hbm.1) | copy-start | bytes 1572868
  6.9 1.0 %copy-start.3 = (bf16[2,6,24,512]{3,2,1,0:T(8,128)(2,1)S(1)}, bf16[2,6,24,512]{3,2,1,0:T(8,128)(2,1)}, u32[]{:S(2)}) copy-start(bf16[2,6,24,512]{3,2,1,0:T(8,128)(2,1)} %param.16) | copy-start | bytes 884740
  7.8 0.9 %copy-start.4 = (s32[288,8]{1,0:T(8,128)S(1)}, s32[288,8]{1,0:T(8,128)}, u32[]{:S(2)}) copy-start(s32[288,8]{1,0:T(8,128)} %constant.8.clone.index_ref) | copy-start | bytes 27652
  8.7 0.9 %copy-start.5 = (bf16[256,256]{1,0:T(8,128)(2,1)S(1)}, bf16[256,256]{1,0:T(8,128)(2,1)}, u32[]{:S(2)}) copy-start(bf16[256,256]{1,0:T(8,128)(2,1)} %constant.7.clone.compact_ref) | copy-start | bytes 393220
  9.6 0.9 %copy-start.6 = (f32[256,2]{1,0:T(8,128)S(1)}, f32[256,2]{1,0:T(8,128)}, u32[]{:S(2)}) copy-start(f32[256,2]{1,0:T(8,128)} %constant.6.clone.coords_ref) | copy-start | bytes 6148
  10.5 0.7 %copy-start.7 = (f32[8,512]{1,0:T(8,128)S(1)}, f32[8,512]{1,0:T(8,128)}, u32[]{:S(2)}) copy-start(f32[8,512]{1,0:T(8,128)} %queries_ref.1) | copy-start | bytes 49156
  11.3 0.7 %copy-start.8 = (f32[3,512]{1,0:T(4,128)S(1)}, f32[3,512]{1,0:T(4,128)}, u32[]{:S(2)}) copy-start(f32[3,512]{1,0:T(4,128)} %first_ref.1) | copy-start | bytes 18436
  12.0 0.7 %copy-start.9 = (f32[512]{0:T(512)S(1)}, f32[512]{0:T(512)}, u32[]{:S(2)}) copy-start(f32[512]{0:T(512)} %param.20) | copy-start | bytes 6148
  12.6 0.7 %copy-start.10 = (f32[512]{0:T(512)S(1)}, f32[512]{0:T(512)}, u32[]{:S(2)}) copy-start(f32[512]{0:T(512)} %param.22) | copy-start | bytes 6148
  13.3 0.7 %copy-start.11 = (f32[512]{0:T(512)S(1)}, f32[512]{0:T(512)}, u32[]{:S(2)}) copy-start(f32[512]{0:T(512)} %param.24) | copy-start | bytes 6148
  14.0 0.7 %copy-start.12 = (s32[8]{0:T(128)S(1)}, s32[8]{0:T(128)}, u32[]{:S(2)}) copy-start(s32[8]{0:T(128)} %order_ref.1) | copy-start | bytes 100

commit v2 on v1

v2 whole, which is shorter than its diff:
```python
import functools
import math

import jax
import jax.numpy as jnp
import numpy as np
from jax import lax
from jax.experimental import pallas as pl
from jax.experimental.pallas import tpu as pltpu
from jax.sharding import PartitionSpec as P

EPSILON = 1e-05
WIDTH = 512
HEADS = 16
HEAD_DIM = WIDTH // HEADS
TOKENS = 144
OWN = 288
TILE = 80
ROW = 24 * TILE
LOG2E = math.log2(math.e)
BF16 = jnp.bfloat16
F32 = jnp.float32


def dot_nn(a, b):
    return lax.dot_general(a, b, (((1,), (0,)), ((), ())), preferred_element_type=F32)


def dot_nt(a, b):
    return lax.dot_general(a, b, (((1,), (1,)), ((), ())), preferred_element_type=F32)


def split(value):
    high = value.astype(BF16)
    return high, (value - high.astype(F32)).astype(BF16)


def coordinate(steps):
    return np.sign(steps) * np.log2(np.abs(steps) + 1.0) / 3.0


def constants():
    place = np.arange(256)
    row, col = place // 23, place % 23
    inside = place < 253
    coords = np.zeros((256, 2), np.float32)
    coords[:, 0] = np.where(inside, coordinate((5 - row) * 8.0 / 5.0), 0.0)
    coords[:, 1] = np.where(inside, coordinate((11 - col) * 8.0 / 11.0), 0.0)
    compact = np.zeros((256, 256), np.float32)
    for part in range(2):
        for k in range(10):
            for x in range(12):
                compact[(k + 1 - part) * 23 + x, part * 128 + 12 * k + x] = 1.0
    index = np.zeros((OWN, 8), np.int32)
    cell = np.arange(OWN)
    block, rest = cell // TOKENS, cell % TOKENS
    index[:, 0] = rest // 12 * 24
    index[:, 1] = block * 12 + rest % 12
    index[:, 2] = cell // 24 * 12
    index[:, 3] = cell % 24
    index[:, 4] = rest % 12
    slot, lat = cell // 24, cell % 24
    index[:48, 5] = (lat // 6 * 48 + slot * 24 + lat % 6 * 4)[:48]
    return coords, compact.astype(BF16), index


def norm(values):
    centre = values - jnp.mean(values, axis=-1, keepdims=True)
    spread = jnp.mean(centre * centre, axis=-1, keepdims=True)
    return centre * lax.rsqrt(spread + EPSILON)


def kernel(
    lon_count,
    lev_count,
    offset_hbm,
    order_hbm,
    latents_hbm,
    wqkv_hbm,
    wproj_hbm,
    wkv_hbm,
    post_gain_hbm,
    first_hbm,
    first_offset_hbm,
    second_hbm,
    dec_gain_hbm,
    head_hbm,
    queries_hbm,
    coords_hbm,
    compact_hbm,
    index_hbm,
    hidden_ref,
    tiles_ref,
    offset_ref,
    order_ref,
    own_ref,
    wqkv_ref,
    wproj_ref,
    wkv_ref,
    post_gain_ref,
    first_ref,
    first_offset_ref,
    second_ref,
    dec_gain_ref,
    head_ref,
    queries_ref,
    coords_ref,
    compact_ref,
    index_ref,
    turned_ref,
    halo_ref,
    shifted_ref,
    lattice_ref,
    bias_ref,
    packed_ref,
    packed_halo_ref,
    attended_ref,
    level_query_ref,
    result_ref,
    send_ref,
    receive_ref,
    local_sem,
    halo_send_sem,
    halo_receive_sem,
    tile_send_sem,
    tile_receive_sem,
):
    lon = lax.axis_index("lon")
    lev = lax.axis_index("lev")
    west = lax.rem(lon + lon_count - 1, lon_count)
    east = lax.rem(lon + 1, lon_count)
    mesh_id = pl.DeviceIdType.MESH

    barrier = pltpu.get_barrier_semaphore()
    for side in (west, east):
        pl.semaphore_signal(barrier, inc=1, device_id=(side, lev), device_id_type=mesh_id)
    for step in range(1, lev_count):
        pl.semaphore_signal(
            barrier,
            inc=1,
            device_id=(lon, lax.rem(lev + step, lev_count)),
            device_id_type=mesh_id,
        )

    loads = {}
    for place, (name, source, target) in enumerate(
        (
            ("index", index_hbm, index_ref),
            ("offset", offset_hbm, offset_ref),
            ("latents", latents_hbm, own_ref),
            ("coords", coords_hbm, coords_ref),
            ("first", first_hbm, first_ref),
            ("first_offset", first_offset_hbm, first_offset_ref),
            ("second", second_hbm, second_ref),
            ("compact", compact_hbm, compact_ref),
            ("wqkv", wqkv_hbm, wqkv_ref),
            ("wproj", wproj_hbm, wproj_ref),
            ("post_gain", post_gain_hbm, post_gain_ref),
            ("dec_gain", dec_gain_hbm, dec_gain_ref),
            ("wkv", wkv_hbm, wkv_ref),
            ("order", order_hbm, order_ref),
            ("queries", queries_hbm, queries_ref),
            ("head", head_hbm, head_ref.at[pl.ds(0, TILE)]),
        )
    ):
        loads[name] = pltpu.make_async_copy(source, target, local_sem.at[place])
        loads[name].start()

    def loaded(*names):
        for name in names:
            loads[name].wait()

    loaded("index", "offset")
    offset = offset_ref[0]
    head_ref[pl.ds(TILE, 128 - TILE), :] = jnp.zeros((128 - TILE, WIDTH), BF16)

    turned_col = index_ref[:, 1:2] + offset
    turned_col = index_ref[:, 0:1] + jnp.where(turned_col >= 24, turned_col - 24, turned_col)
    cells = lax.broadcasted_iota(jnp.int32, (OWN, OWN), 1)
    turn = jnp.where(cells == turned_col, 1.0, 0.0).astype(BF16)
    loaded("latents")
    turned_ref[...] = dot_nn(turn, own_ref[...]).astype(BF16)

    pl.semaphore_wait(barrier, 2 + lev_count - 1)
    halo_copies = []
    for place, side in enumerate((east, west)):
        copy = pltpu.make_async_remote_copy(
            src_ref=turned_ref.at[pl.ds(TOKENS, TOKENS)],
            dst_ref=halo_ref.at[place],
            send_sem=halo_send_sem.at[place],
            recv_sem=halo_receive_sem.at[place],
            device_id=(side, lev),
            device_id_type=mesh_id,
        )
        copy.start()
        halo_copies.append(copy)

    lane24 = lax.broadcasted_iota(jnp.int32, (24, 128), 1)
    loaded("coords", "first", "first_offset", "second", "compact")
    second_high, second_low = split(second_ref[...])
    second_both = jnp.concatenate([second_high, second_low], axis=0)
    flat_part = (
        coords_ref[:, 0:1] * first_ref[1:2, :]
        + coords_ref[:, 1:2] * first_ref[2:3, :]
        + first_offset_ref[...]
    )
    for a in range(3):
        depth_coord = float(coordinate(np.float64((1 - a) * 8.0)))
        hidden = jnp.maximum(flat_part + depth_coord * first_ref[0:1, :], 0.0)
        hidden_high, hidden_low = split(hidden)
        both = dot_nt(second_both, hidden_high)
        logits = both[:HEADS] + both[HEADS:] + dot_nt(second_high, hidden_low)
        table = (16.0 * LOG2E) / (1.0 + jnp.exp(-logits))
        for x in range(12):
            rolled = table if x == 11 else pltpu.roll(table, 256 - (11 - x), 1)
            high, low = split(rolled)
            shifted_ref[pl.ds(x * HEADS, HEADS), :] = high
            shifted_ref[pl.ds((12 + x) * HEADS, HEADS), :] = low
        spread_out = dot_nn(shifted_ref[...], compact_ref[...])
        spread_out = spread_out[:192] + spread_out[192:]
        lattice_ref[a, pl.ds(0, 192), :] = spread_out[:, :128]
        lattice_ref[a, pl.ds(192, 192), :] = spread_out[:, 128:]

    for h in range(HEADS):
        lattice = [lattice_ref[a, pl.ds(h, 24, stride=HEADS), :] for a in range(3)]
        for dz in range(2):
            for m in range(3):
                start = (4 - 2 * m) * 12
                rows = pl.ds(72 * dz + 24 * m, 24)
                near = lattice[1 - dz]
                if start:
                    near = pltpu.roll(near, 128 - start, 1)
                far = pltpu.roll(lattice[2 - dz], 72 - start, 1)
                bias_ref[h, rows, :128] = jnp.where(lane24 < 72, near, far)
                bias_ref[h, rows, 128:] = far[:, :16]

    loaded("wqkv")
    turned = turned_ref[...]
    scale = LOG2E / math.sqrt(HEAD_DIM)
    packed_ref[:, :WIDTH] = (dot_nn(turned, wqkv_ref[:, :WIDTH]) * scale).astype(BF16)
    packed_ref[:, WIDTH:] = dot_nn(turned, wqkv_ref[:, WIDTH:]).astype(BF16)

    def soft(scores):
        raised = jnp.exp2(scores - jnp.max(scores, axis=-1, keepdims=True))
        total = jnp.sum(raised, axis=-1, keepdims=True)
        return (raised * pl.reciprocal(total, approx=True)).astype(BF16)

    lane128 = lax.broadcasted_iota(jnp.int32, (TOKENS, 128), 1)
    inner = pl.ds(0, TOKENS)
    zero = jnp.zeros((), BF16)
    for quad in range(4):
        q_inner = packed_ref[inner, pl.ds(128 * quad, 128)]
        k_inner = packed_ref[inner, pl.ds(WIDTH + 128 * quad, 128)]
        v_inner = packed_ref[inner, pl.ds(2 * WIDTH + 128 * quad, 128)]
        out = jnp.zeros((TOKENS, 128), F32)
        for j in range(4):
            mine = lane128 // HEAD_DIM == j
            weights = soft(dot_nt(jnp.where(mine, q_inner, zero), k_inner) + bias_ref[4 * quad + j])
            out = jnp.where(mine, dot_nn(weights, v_inner), out)
        attended_ref[inner, pl.ds(128 * quad, 128)] = out.astype(BF16)

    for copy in halo_copies:
        copy.wait()
    upper = index_ref[:TOKENS, 4:5] >= 12 - offset
    halo = jnp.where(upper, halo_ref[1].astype(F32), halo_ref[0].astype(F32)).astype(BF16)
    packed_halo_ref[...] = dot_nn(halo, wqkv_ref[:, WIDTH:]).astype(BF16)
    lane256 = lax.broadcasted_iota(jnp.int32, (TOKENS, 256), 1)
    edge = pl.ds(TOKENS, TOKENS)
    for quad in range(4):
        q_edge = packed_ref[edge, pl.ds(128 * quad, 128)].astype(F32)
        k_edge = packed_ref[edge, pl.ds(WIDTH + 128 * quad, 128)].astype(F32)
        v_edge = packed_ref[edge, pl.ds(2 * WIDTH + 128 * quad, 128)].astype(F32)
        k_halo = packed_halo_ref[:, pl.ds(128 * quad, 128)].astype(F32)
        v_halo = packed_halo_ref[:, pl.ds(WIDTH + 128 * quad, 128)].astype(F32)
        q_both = jnp.concatenate([jnp.where(upper, q_edge, 0.0), jnp.where(upper, 0.0, q_edge)], 1)
        k_both = jnp.concatenate(
            [jnp.where(upper, k_edge, k_halo), jnp.where(upper, k_halo, k_edge)], 1
        )
        v_both = jnp.concatenate(
            [jnp.where(upper, v_edge, v_halo), jnp.where(upper, v_halo, v_edge)], 1
        )
        q_both, k_both, v_both = q_both.astype(BF16), k_both.astype(BF16), v_both.astype(BF16)
        out_upper = jnp.zeros((TOKENS, 128), F32)
        out_lower = jnp.zeros((TOKENS, 128), F32)
        for j in range(4):
            mine = lane256 % 128 // HEAD_DIM == j
            weights = soft(dot_nt(jnp.where(mine, q_both, zero), k_both) + bias_ref[4 * quad + j])
            both = dot_nn(weights, v_both)
            mine = lane128 // HEAD_DIM == j
            out_upper = jnp.where(mine, both[:, :128], out_upper)
            out_lower = jnp.where(mine, both[:, 128:], out_lower)
        out = jnp.where(upper, out_upper, out_lower)
        attended_ref[edge, pl.ds(128 * quad, 128)] = out.astype(BF16)

    loaded("wproj", "post_gain", "dec_gain")
    projected = dot_nn(attended_ref[...], wproj_ref[...])
    mixed = (turned_ref[...].astype(F32) + post_gain_ref[...] * norm(projected)).astype(BF16)
    back_col = index_ref[:, 3:4] - offset
    back_col = jnp.where(back_col < 0, back_col + 24, back_col)
    back_col = index_ref[:, 2:3] + jnp.where(back_col >= 12, back_col + (TOKENS - 12), back_col)
    turn_back = jnp.where(cells == back_col, 1.0, 0.0).astype(BF16)
    state = dot_nn(turn_back, mixed)
    hidden_ref[...] = state.astype(BF16)

    normed = (dec_gain_ref[...] * norm(state)).astype(BF16)
    loaded("wkv", "order", "queries", "head")
    keys = dot_nn(normed, wkv_ref[:, :WIDTH]).astype(BF16)
    values = dot_nn(normed, wkv_ref[:, WIDTH:]).astype(BF16).astype(F32)
    head_lane = lax.broadcasted_iota(jnp.int32, (HEADS, WIDTH), 1) // HEAD_DIM
    head_row = lax.broadcasted_iota(jnp.int32, (HEADS, WIDTH), 0)
    for i in range(8):
        query = queries_ref[pl.ds(order_ref[i], 1), :]
        level_query_ref[pl.ds(i * HEADS, HEADS), :] = jnp.where(
            head_lane == head_row, query, 0.0
        ).astype(BF16)
    scores = dot_nt(keys, level_query_ref[...]) * (0.5 / math.sqrt(HEAD_DIM))
    upper_weight = 0.5 + 0.5 * jnp.tanh(scores[:TOKENS] - scores[TOKENS:])
    weight_high, weight_low = split(upper_weight)
    weight_both = jnp.concatenate([weight_high, weight_low], axis=1)
    expand = jnp.where(
        lax.broadcasted_iota(jnp.int32, (256, WIDTH), 0) % HEADS
        == lax.broadcasted_iota(jnp.int32, (256, WIDTH), 1) // HEAD_DIM,
        1.0,
        0.0,
    ).astype(BF16)
    level_lane = lane256 % 128 // HEADS
    value_lower = values[TOKENS:]
    value_step = values[:TOKENS] - value_lower
    lane48 = lax.broadcasted_iota(jnp.int32, (48, 128), 1)

    def piece(parts):
        tile = parts[0][1]
        for start, part in parts[1:]:
            tile = jnp.where(lane48 >= start, part, tile)
        return tile

    tile_copies = []
    for step in (2, 3, 1, 0):
        target = lax.rem(lev + step, lev_count)
        for j in range(2):
            wide = dot_nn(jnp.where(level_lane == 2 * target + j, weight_both, zero), expand)
            decoded = (value_lower + wide * value_step).astype(BF16)
            result_ref[step, pl.ds(j * TOKENS, TOKENS), :] = dot_nt(decoded, head_ref[...])
        slabs = []
        for x in range(6):
            slab = result_ref[step, pl.ds(x, 48, stride=6), :]
            slabs.append(pltpu.roll(slab, x * TILE % 128, 1) if x * TILE % 128 else slab)
        block = jnp.concatenate(
            [
                piece([(TILE * x - 128 * k, slabs[x]) for x in range(128 * k // TILE, min((128 * k + 127) // TILE, 5) + 1)])
                for k in range(4)
            ],
            axis=1,
        ).astype(BF16)
        if step == 0:
            receive_ref[pl.ds(lev, 1)] = block[None]
            continue
        send_ref[step - 1] = block
        copy = pltpu.make_async_remote_copy(
            src_ref=send_ref.at[step - 1],
            dst_ref=receive_ref.at[lev],
            send_sem=tile_send_sem.at[step - 1],
            recv_sem=tile_receive_sem.at[step - 1],
            device_id=(lon, target),
            device_id_type=mesh_id,
        )
        copy.start()
        tile_copies.append(copy)

    rows = 48 * lev_count
    place = lax.broadcasted_iota(jnp.int32, (48, rows), 1) - index_ref[:48, 5:6]
    gather = jnp.concatenate([jnp.where(place == q, 1.0, 0.0) for q in range(4)], 0).astype(BF16)
    for copy in tile_copies:
        copy.wait()
    sorted_rows = dot_nn(gather, receive_ref[...].reshape(rows, WIDTH))
    parts = [[] for _ in range(ROW // 128)]
    for q in range(4):
        for c in range(4):
            part = sorted_rows[48 * q : 48 * q + 48, 128 * c : 128 * c + 128]
            if 480 * q % 128:
                part = pltpu.roll(part, 480 * q % 128, 1)
            first = 480 * q + 128 * c
            last = min(first + 128, 480 * q + 480) - 1
            for k in range(first // 128, last // 128 + 1):
                parts[k].append((first - 128 * k, part))
    for k in range(ROW // 128):
        tiles_ref[:, pl.ds(128 * k, 128)] = piece(parts[k]).astype(BF16)


def body(
    latents,
    shift_offset,
    qkv_weight,
    proj_weight,
    post_gain,
    bias_first_weight,
    bias_first_offset,
    bias_second_weight,
    dec_gain,
    kv_weight,
    head_weight,
    level_queries,
    level_order,
):
    lon_count = lax.axis_size("lon")
    lev_count = lax.axis_size("lev")
    coords, compact, index = constants()
    vmem = pl.BlockSpec(memory_space=pltpu.VMEM)
    hbm = pl.BlockSpec(memory_space=pltpu.HBM)
    dma = pltpu.SemaphoreType.DMA
    hidden, tiles = pl.pallas_call(
        functools.partial(kernel, lon_count, lev_count),
        out_shape=(
            jax.ShapeDtypeStruct((OWN, WIDTH), BF16),
            jax.ShapeDtypeStruct((48, ROW), BF16),
        ),
        in_specs=[hbm] * 16,
        out_specs=(vmem, vmem),
        scratch_shapes=[
            pltpu.SMEM((1,), jnp.int32),
            pltpu.SMEM((8,), jnp.int32),
            pltpu.VMEM((OWN, WIDTH), BF16),
            pltpu.VMEM((WIDTH, 3 * WIDTH), BF16),
            pltpu.VMEM((WIDTH, WIDTH), BF16),
            pltpu.VMEM((WIDTH, 2 * WIDTH), BF16),
            pltpu.VMEM((1, WIDTH), F32),
            pltpu.VMEM((3, WIDTH), F32),
            pltpu.VMEM((1, WIDTH), F32),
            pltpu.VMEM((HEADS, WIDTH), F32),
            pltpu.VMEM((1, WIDTH), F32),
            pltpu.VMEM((128, WIDTH), BF16),
            pltpu.VMEM((8, WIDTH), F32),
            pltpu.VMEM((256, 2), F32),
            pltpu.VMEM((256, 256), BF16),
            pltpu.VMEM((OWN, 8), jnp.int32),
            pltpu.VMEM((OWN, WIDTH), BF16),
            pltpu.VMEM((2, TOKENS, WIDTH), BF16),
            pltpu.VMEM((384, 256), BF16),
            pltpu.VMEM((3, 384, 128), F32),
            pltpu.VMEM((HEADS, TOKENS, TOKENS), F32),
            pltpu.VMEM((OWN, 3 * WIDTH), BF16),
            pltpu.VMEM((TOKENS, 2 * WIDTH), BF16),
            pltpu.VMEM((OWN, WIDTH), BF16),
            pltpu.VMEM((128, WIDTH), BF16),
            pltpu.VMEM((lev_count, 2 * TOKENS, 128), F32),
            pltpu.VMEM((lev_count - 1, 48, WIDTH), BF16),
            pltpu.VMEM((lev_count, 48, WIDTH), BF16),
            dma((16,)),
            dma((2,)),
            dma((2,)),
            dma((lev_count - 1,)),
            dma((lev_count - 1,)),
        ],
        compiler_params=pltpu.CompilerParams(
            collective_id=0, has_side_effects=True, vmem_limit_bytes=40 * 1024 * 1024
        ),
    )(
        shift_offset,
        *(
            pltpu.with_memory_space_constraint(value, pltpu.HBM)
            for value in (
                level_order,
                latents.reshape(OWN, WIDTH),
                qkv_weight,
                proj_weight,
                kv_weight,
                post_gain.reshape(1, WIDTH),
                bias_first_weight,
                bias_first_offset.reshape(1, WIDTH),
                bias_second_weight.T,
                dec_gain.reshape(1, WIDTH),
                head_weight.T,
                level_queries,
                jnp.asarray(coords),
                jnp.asarray(compact),
                jnp.asarray(index),
            )
        )
    )
    return hidden.reshape(latents.shape), tiles.reshape(2, 24, ROW)


def solution(mesh):
    return jax.shard_map(
        body,
        mesh=mesh,
        in_specs=(P(None, "lev", "lon", None),) + (P(),) * 12,
        out_specs=(P(None, "lev", "lon", None), P("lev", None, "lon")),
        check_vma=False,
    )
```

time: 50.7 us -> 30.3 us (0.60)
  local copies, waits for them, and re-layouts: 14.7 us -> 1.39 us
  Pallas kernels: 34 us -> 27.5 us
    unnamed x30 -> x2, local copies, waits for them, and re-layouts: 14.7 us -> 1.39 us
    pallas_call x1, Pallas kernels: 34 us -> 27.5 us  [body(): pl.pallas_call(functools.partial(kernel, lon_count, lev_count), out_shape...]
where the time goes in v2:
time: 30.3 us; the launch traced here: 30.2 us
  Pallas kernels  27.5 us (91%)
  local copies, waits for them, and re-layouts  1.39 us (5%)
  between operations  1.29 us (4%)
    pallas_call x1, Pallas kernels, body(): pl.pallas_call(functools.partial(kernel, lon_count, lev_count), out_shape...  27.5 us
    unnamed x2, local copies, waits for them, and re-layouts  1.39 us

profile of v2, /device:TPU:64, one launch (start us, length us, event | category | flops | bytes accessed | tf_op | source)
XLA Modules:
  0.0 30.2 jit_solution(4656075440196965137)
XLA Ops:
  1.3 27.5 %shard_map.167 = (bf16[288,512]{1,0:T(8,128)(2,1)S(1)}, bf16[48,1920]{1,0:T(8,128)(2,1)S(1)}) custom-call(s32[1]{0:T(128)S(6)} %copy.20.offset_hbm, s32[8]{0:T(128)} %order_hbm.1, bf16[288,512]{1,0:T(8,128)(2,1)} %bitcast.10, bf16[512,1536]{1,0:T(8,128)(2,1)} %wqkv_hbm.1, bf16[512,512]{1,0:T(8,128)(2,1)} %wproj_hbm.1, bf16[512,1024]{1,0:T(8,128)(2,1)} %wkv_hbm.1, ...), custom_call_target="tpu_custom_call" | custom-call | tf_op jit(solution)/shard_map/pallas_call | solution.py:411
  28.8 0.7 %copy.21 = bf16[2,6,24,512]{3,2,1,0:T(8,128)(2,1)} copy(bf16[2,6,24,512]{3,2,1,0:T(8,128)(2,1)S(1)} %bitcast.8) | data formatting | bytes 589824
  29.5 0.7 %copy.22 = bf16[2,24,1920]{2,1,0:T(8,128)(2,1)} copy(bf16[2,24,1920]{2,1,0:T(8,128)(2,1)S(1)} %bitcast.9) | data formatting | bytes 368640

commit v3 on v2

--- a/solution.py
+++ b/solution.py
@@ -51,17 +51,11 @@
         for k in range(10):
             for x in range(12):
                 compact[(k + 1 - part) * 23 + x, part * 128 + 12 * k + x] = 1.0
-    index = np.zeros((OWN, 8), np.int32)
-    cell = np.arange(OWN)
-    block, rest = cell // TOKENS, cell % TOKENS
-    index[:, 0] = rest // 12 * 24
-    index[:, 1] = block * 12 + rest % 12
-    index[:, 2] = cell // 24 * 12
-    index[:, 3] = cell % 24
-    index[:, 4] = rest % 12
-    slot, lat = cell // 24, cell % 24
-    index[:48, 5] = (lat // 6 * 48 + slot * 24 + lat % 6 * 4)[:48]
-    return coords, compact.astype(BF16), index
+    return coords, compact.astype(BF16)
+
+
+def over_twelve(value):
+    return lax.shift_right_logical(value * 43691, 19)
 
 
 def norm(values):
@@ -88,7 +82,6 @@
     queries_hbm,
     coords_hbm,
     compact_hbm,
-    index_hbm,
     hidden_ref,
     tiles_ref,
     offset_ref,
@@ -106,7 +99,6 @@
     queries_ref,
     coords_ref,
     compact_ref,
-    index_ref,
     turned_ref,
     halo_ref,
     shifted_ref,
@@ -115,7 +107,9 @@
     packed_ref,
     packed_halo_ref,
     attended_ref,
+    mixed_ref,
     level_query_ref,
+    expand_ref,
     result_ref,
     send_ref,
     receive_ref,
@@ -145,7 +139,6 @@
     loads = {}
     for place, (name, source, target) in enumerate(
         (
-            ("index", index_hbm, index_ref),
             ("offset", offset_hbm, offset_ref),
             ("latents", latents_hbm, own_ref),
             ("coords", coords_hbm, coords_ref),
@@ -170,12 +163,17 @@
         for name in names:
             loads[name].wait()
 
-    loaded("index", "offset")
+    loaded("offset")
     offset = offset_ref[0]
     head_ref[pl.ds(TILE, 128 - TILE), :] = jnp.zeros((128 - TILE, WIDTH), BF16)
 
-    turned_col = index_ref[:, 1:2] + offset
-    turned_col = index_ref[:, 0:1] + jnp.where(turned_col >= 24, turned_col - 24, turned_col)
+    cell = lax.broadcasted_iota(jnp.int32, (OWN, 1), 0)
+    rest = jnp.where(cell >= TOKENS, cell - TOKENS, cell)
+    line = over_twelve(rest)
+    col = rest - 12 * line
+    upper = col[:TOKENS] >= 12 - offset
+    turned_col = col + jnp.where(cell >= TOKENS, 12, 0) + offset
+    turned_col = 24 * line + jnp.where(turned_col >= 24, turned_col - 24, turned_col)
     cells = lax.broadcasted_iota(jnp.int32, (OWN, OWN), 1)
     turn = jnp.where(cells == turned_col, 1.0, 0.0).astype(BF16)
     loaded("latents")
@@ -245,6 +243,87 @@
         total = jnp.sum(raised, axis=-1, keepdims=True)
         return (raised * pl.reciprocal(total, approx=True)).astype(BF16)
 
+    loaded("wproj", "post_gain", "dec_gain", "wkv", "order", "queries", "head")
+    head_lane = lax.broadcasted_iota(jnp.int32, (HEADS, WIDTH), 1) // HEAD_DIM
+    head_row = lax.broadcasted_iota(jnp.int32, (HEADS, WIDTH), 0)
+    for i in range(8):
+        query = queries_ref[pl.ds(order_ref[i], 1), :]
+        level_query_ref[pl.ds(i * HEADS, HEADS), :] = jnp.where(
+            head_lane == head_row, query, 0.0
+        ).astype(BF16)
+    expand_ref[...] = jnp.where(
+        lax.broadcasted_iota(jnp.int32, (256, WIDTH), 0) % HEADS
+        == lax.broadcasted_iota(jnp.int32, (256, WIDTH), 1) // HEAD_DIM,
+        1.0,
+        0.0,
+    ).astype(BF16)
+    lane48 = lax.broadcasted_iota(jnp.int32, (48, 128), 1)
+    level_lane = lax.broadcasted_iota(jnp.int32, (72, 256), 1) % 128 // HEADS
+    tile_copies = ([], [])
+
+    def piece(parts):
+        tile = parts[0][1]
+        for start, part in parts[1:]:
+            tile = jnp.where(lane48 >= start, part, tile)
+        return tile
+
+    def finish(half, groups):
+        mine = pl.ds(TOKENS * half, TOKENS)
+        projected = dot_nn(attended_ref[mine, :], wproj_ref[...])
+        mixed = (turned_ref[mine, :].astype(F32) + post_gain_ref[...] * norm(projected)).astype(BF16)
+        mixed_ref[mine, :] = mixed
+        normed = (dec_gain_ref[...] * norm(mixed.astype(F32))).astype(BF16)
+        keys = dot_nn(normed, wkv_ref[:, :WIDTH]).astype(BF16)
+        values = dot_nn(normed, wkv_ref[:, WIDTH:]).astype(BF16).astype(F32)
+        scores = dot_nt(keys, level_query_ref[...]) * (0.5 / math.sqrt(HEAD_DIM))
+        upper_weight = 0.5 + 0.5 * jnp.tanh(scores[:72] - scores[72:])
+        weight_high = upper_weight.astype(BF16).astype(F32)
+        weight_both = jnp.concatenate([weight_high, upper_weight - weight_high], axis=1)
+        value_lower = values[72:]
+        value_step = values[:72] - value_lower
+        for group in groups:
+            targets = [lax.rem(lev + step, lev_count) for step in group]
+            levels = [2 * target + j for target in targets for j in range(2)]
+            picked = jnp.concatenate(
+                [jnp.where(level_lane == level, weight_both, 0.0) for level in levels], axis=0
+            ).astype(BF16)
+            wide = dot_nn(picked, expand_ref[...])
+            decoded = jnp.concatenate(
+                [
+                    value_lower + wide[72 * i : 72 * i + 72] * value_step
+                    for i in range(len(levels))
+                ],
+                axis=0,
+            ).astype(BF16)
+            result = dot_nt(decoded, head_ref[...])
+            for i, step in enumerate(group):
+                result_ref[half, step] = result[TOKENS * i : TOKENS * i + TOKENS]
+                slabs = []
+                for x in range(3):
+                    slab = result_ref[half, step, pl.ds(x, 48, stride=3), :]
+                    slabs.append(pltpu.roll(slab, x * TILE % 128, 1) if x else slab)
+                block = jnp.concatenate(
+                    [
+                        piece([(0, slabs[0]), (TILE, slabs[1])]),
+                        piece([(0, slabs[1]), (2 * TILE - 128, slabs[2])]),
+                    ],
+                    axis=1,
+                ).astype(BF16)
+                if step == 0:
+                    receive_ref[half, pl.ds(lev, 1)] = block[None]
+                    continue
+                send_ref[half, step - 1] = block
+                copy = pltpu.make_async_remote_copy(
+                    src_ref=send_ref.at[half, step - 1],
+                    dst_ref=receive_ref.at[half, lev],
+                    send_sem=tile_send_sem.at[half, step - 1],
+                    recv_sem=tile_receive_sem.at[half, step - 1],
+                    device_id=(lon, targets[i]),
+                    device_id_type=mesh_id,
+                )
+                copy.start()
+                tile_copies[half].append(copy)
+
     lane128 = lax.broadcasted_iota(jnp.int32, (TOKENS, 128), 1)
     inner = pl.ds(0, TOKENS)
     zero = jnp.zeros((), BF16)
@@ -259,9 +338,10 @@
             out = jnp.where(mine, dot_nn(weights, v_inner), out)
         attended_ref[inner, pl.ds(128 * quad, 128)] = out.astype(BF16)
 
+    finish(0, ((2, 3, 1, 0),))
+
     for copy in halo_copies:
         copy.wait()
-    upper = index_ref[:TOKENS, 4:5] >= 12 - offset
     halo = jnp.where(upper, halo_ref[1].astype(F32), halo_ref[0].astype(F32)).astype(BF16)
     packed_halo_ref[...] = dot_nn(halo, wqkv_ref[:, WIDTH:]).astype(BF16)
     lane256 = lax.broadcasted_iota(jnp.int32, (TOKENS, 256), 1)
@@ -292,99 +372,55 @@
         out = jnp.where(upper, out_upper, out_lower)
         attended_ref[edge, pl.ds(128 * quad, 128)] = out.astype(BF16)
 
-    loaded("wproj", "post_gain", "dec_gain")
-    projected = dot_nn(attended_ref[...], wproj_ref[...])
-    mixed = (turned_ref[...].astype(F32) + post_gain_ref[...] * norm(projected)).astype(BF16)
-    back_col = index_ref[:, 3:4] - offset
+    finish(1, ((2, 3), (1, 0)))
+
+    own_line = over_twelve(lax.shift_right_logical(cell, 1))
+    back_col = cell - 24 * own_line - offset
     back_col = jnp.where(back_col < 0, back_col + 24, back_col)
-    back_col = index_ref[:, 2:3] + jnp.where(back_col >= 12, back_col + (TOKENS - 12), back_col)
+    back_col = 12 * own_line + jnp.where(back_col >= 12, back_col + (TOKENS - 12), back_col)
     turn_back = jnp.where(cells == back_col, 1.0, 0.0).astype(BF16)
-    state = dot_nn(turn_back, mixed)
-    hidden_ref[...] = state.astype(BF16)
-
-    normed = (dec_gain_ref[...] * norm(state)).astype(BF16)
-    loaded("wkv", "order", "queries", "head")
-    keys = dot_nn(normed, wkv_ref[:, :WIDTH]).astype(BF16)
-    values = dot_nn(normed, wkv_ref[:, WIDTH:]).astype(BF16).astype(F32)
-    head_lane = lax.broadcasted_iota(jnp.int32, (HEADS, WIDTH), 1) // HEAD_DIM
-    head_row = lax.broadcasted_iota(jnp.int32, (HEADS, WIDTH), 0)
-    for i in range(8):
-        query = queries_ref[pl.ds(order_ref[i], 1), :]
-        level_query_ref[pl.ds(i * HEADS, HEADS), :] = jnp.where(
-            head_lane == head_row, query, 0.0
-        ).astype(BF16)
-    scores = dot_nt(keys, level_query_ref[...]) * (0.5 / math.sqrt(HEAD_DIM))
-    upper_weight = 0.5 + 0.5 * jnp.tanh(scores[:TOKENS] - scores[TOKENS:])
-    weight_high, weight_low = split(upper_weight)
-    weight_both = jnp.concatenate([weight_high, weight_low], axis=1)
-    expand = jnp.where(
-        lax.broadcasted_iota(jnp.int32, (256, WIDTH), 0) % HEADS
-        == lax.broadcasted_iota(jnp.int32, (256, WIDTH), 1) // HEAD_DIM,
-        1.0,
-        0.0,
-    ).astype(BF16)
-    level_lane = lane256 % 128 // HEADS
-    value_lower = values[TOKENS:]
-    value_step = values[:TOKENS] - value_lower
-    lane48 = lax.broadcasted_iota(jnp.int32, (48, 128), 1)
-
-    def piece(parts):
-        tile = parts[0][1]
-        for start, part in parts[1:]:
-            tile = jnp.where(lane48 >= start, part, tile)
-        return tile
-
-    tile_copies = []
-    for step in (2, 3, 1, 0):
-        target = lax.rem(lev + step, lev_count)
-        for j in range(2):
-            wide = dot_nn(jnp.where(level_lane == 2 * target + j, weight_both, zero), expand)
-            decoded = (value_lower + wide * value_step).astype(BF16)
-            result_ref[step, pl.ds(j * TOKENS, TOKENS), :] = dot_nt(decoded, head_ref[...])
-        slabs = []
-        for x in range(6):
-            slab = result_ref[step, pl.ds(x, 48, stride=6), :]
-            slabs.append(pltpu.roll(slab, x * TILE % 128, 1) if x * TILE % 128 else slab)
-        block = jnp.concatenate(
-            [
-                piece([(TILE * x - 128 * k, slabs[x]) for x in range(128 * k // TILE, min((128 * k + 127) // TILE, 5) + 1)])
-                for k in range(4)
-            ],
-            axis=1,
-        ).astype(BF16)
-        if step == 0:
-            receive_ref[pl.ds(lev, 1)] = block[None]
-            continue
-        send_ref[step - 1] = block
-        copy = pltpu.make_async_remote_copy(
-            src_ref=send_ref.at[step - 1],
-            dst_ref=receive_ref.at[lev],
-            send_sem=tile_send_sem.at[step - 1],
-            recv_sem=tile_receive_sem.at[step - 1],
-            device_id=(lon, target),
-            device_id_type=mesh_id,
-        )
-        copy.start()
-        tile_copies.append(copy)
+    hidden_ref[...] = dot_nn(turn_back, mixed_ref[...]).astype(BF16)
 
     rows = 48 * lev_count
-    place = lax.broadcasted_iota(jnp.int32, (48, rows), 1) - index_ref[:48, 5:6]
+    slot_row = lax.broadcasted_iota(jnp.int32, (48, 1), 0)
+    slot = jnp.where(slot_row >= 24, 1, 0)
+    lat = slot_row - 24 * slot
+    source = over_twelve(2 * lat)
+    base = 48 * source + 24 * slot + 4 * (lat - 6 * source)
+    place = lax.broadcasted_iota(jnp.int32, (48, rows), 1) - base
     gather = jnp.concatenate([jnp.where(place == q, 1.0, 0.0) for q in range(4)], 0).astype(BF16)
-    for copy in tile_copies:
-        copy.wait()
-    sorted_rows = dot_nn(gather, receive_ref[...].reshape(rows, WIDTH))
     parts = [[] for _ in range(ROW // 128)]
-    for q in range(4):
-        for c in range(4):
-            part = sorted_rows[48 * q : 48 * q + 48, 128 * c : 128 * c + 128]
-            if 480 * q % 128:
-                part = pltpu.roll(part, 480 * q % 128, 1)
-            first = 480 * q + 128 * c
-            last = min(first + 128, 480 * q + 480) - 1
-            for k in range(first // 128, last // 128 + 1):
-                parts[k].append((first - 128 * k, part))
-    for k in range(ROW // 128):
-        tiles_ref[:, pl.ds(128 * k, 128)] = piece(parts[k]).astype(BF16)
+    for half in range(2):
+        for copy in tile_copies[half]:
+            copy.wait()
+        sorted_rows = dot_nn(gather, receive_ref[half].reshape(rows, 256))
+        for q in range(4):
+            for c in range(2):
+                part = sorted_rows[48 * q : 48 * q + 48, 128 * c : 128 * c + 128]
+                first = 960 * half + 240 * q + 128 * c
+                if first % 128:
+                    part = pltpu.roll(part, first % 128, 1)
+                last = first + (127 if c == 0 else 111)
+                for k in range(first // 128, last // 128 + 1):
+                    parts[k].append((first - 128 * k, part))
+    shift = TILE * offset
+    count = ROW // 128
+    tiles = [piece(part).astype(BF16) for part in parts]
+    pairs = jnp.concatenate(
+        [jnp.concatenate([tiles[k - 1], tiles[k]], axis=1) for k in range(count)], axis=0
+    )
+    slide = lax.broadcasted_iota(jnp.int32, (256, 128), 0) - lax.broadcasted_iota(
+        jnp.int32, (256, 128), 1
+    )
+    slide = jnp.where(slide == 128 - (shift & 127), 1.0, 0.0).astype(BF16)
+    turned_lanes = dot_nn(pairs, slide)
+    tiles = [turned_lanes[48 * k : 48 * k + 48] for k in range(count)]
+    whole = jnp.zeros((48, 128), jnp.int32) + lax.shift_right_logical(shift, 7)
+    for bit in (1, 2, 4):
+        chosen = whole & bit != 0
+        tiles = [jnp.where(chosen, tiles[k - bit], tiles[k]) for k in range(count)]
+    for k in range(count):
+        tiles_ref[:, pl.ds(128 * k, 128)] = tiles[k].astype(BF16)
 
 
 def body(
@@ -404,7 +440,7 @@
 ):
     lon_count = lax.axis_size("lon")
     lev_count = lax.axis_size("lev")
-    coords, compact, index = constants()
+    coords, compact = constants()
     vmem = pl.BlockSpec(memory_space=pltpu.VMEM)
     hbm = pl.BlockSpec(memory_space=pltpu.HBM)
     dma = pltpu.SemaphoreType.DMA
@@ -414,7 +450,7 @@
             jax.ShapeDtypeStruct((OWN, WIDTH), BF16),
             jax.ShapeDtypeStruct((48, ROW), BF16),
         ),
-        in_specs=[hbm] * 16,
+        in_specs=[hbm] * 15,
         out_specs=(vmem, vmem),
         scratch_shapes=[
             pltpu.SMEM((1,), jnp.int32),
@@ -432,7 +468,6 @@
             pltpu.VMEM((8, WIDTH), F32),
             pltpu.VMEM((256, 2), F32),
             pltpu.VMEM((256, 256), BF16),
-            pltpu.VMEM((OWN, 8), jnp.int32),
             pltpu.VMEM((OWN, WIDTH), BF16),
             pltpu.VMEM((2, TOKENS, WIDTH), BF16),
             pltpu.VMEM((384, 256), BF16),
@@ -441,15 +476,17 @@
             pltpu.VMEM((OWN, 3 * WIDTH), BF16),
             pltpu.VMEM((TOKENS, 2 * WIDTH), BF16),
             pltpu.VMEM((OWN, WIDTH), BF16),
+            pltpu.VMEM((OWN, WIDTH), BF16),
             pltpu.VMEM((128, WIDTH), BF16),
-            pltpu.VMEM((lev_count, 2 * TOKENS, 128), F32),
-            pltpu.VMEM((lev_count - 1, 48, WIDTH), BF16),
-            pltpu.VMEM((lev_count, 48, WIDTH), BF16),
-            dma((16,)),
+            pltpu.VMEM((256, WIDTH), BF16),
+            pltpu.VMEM((2, lev_count, TOKENS, 128), F32),
+            pltpu.VMEM((2, lev_count - 1, 48, 256), BF16),
+            pltpu.VMEM((2, lev_count, 48, 256), BF16),
+            dma((15,)),
             dma((2,)),
             dma((2,)),
-            dma((lev_count - 1,)),
-            dma((lev_count - 1,)),
+            dma((2, lev_count - 1)),
+            dma((2, lev_count - 1)),
         ],
         compiler_params=pltpu.CompilerParams(
             collective_id=0, has_side_effects=True, vmem_limit_bytes=40 * 1024 * 1024
@@ -473,7 +510,6 @@
                 level_queries,
                 jnp.asarray(coords),
                 jnp.asarray(compact),
-                jnp.asarray(index),
             )
         )
     )

time: 30.3 us -> 30.5 us (level)
  no operation moved by 1% of the time
where the time goes in v3:
time: 30.5 us; the launch traced here: 30.4 us
  Pallas kernels  27.7 us (91%)
  local copies, waits for them, and re-layouts  1.39 us (5%)
  between operations  1.29 us (4%)
    pallas_call x1, Pallas kernels, body(): pl.pallas_call(functools.partial(kernel, lon_count, lev_count), out_shape...  27.7 us
    unnamed x2, local copies, waits for them, and re-layouts  1.39 us

profile of v3, /device:TPU:64, one launch (start us, length us, event | category | flops | bytes accessed | tf_op | source)
XLA Modules:
  0.0 30.4 jit_solution(4985718646996693837)
XLA Ops:
  1.3 27.7 %shard_map.158 = (bf16[288,512]{1,0:T(8,128)(2,1)S(1)}, bf16[48,1920]{1,0:T(8,128)(2,1)S(1)}) custom-call(s32[1]{0:T(128)S(6)} %copy.19.offset_hbm, s32[8]{0:T(128)} %order_hbm.1, bf16[288,512]{1,0:T(8,128)(2,1)} %bitcast.10, bf16[512,1536]{1,0:T(8,128)(2,1)} %wqkv_hbm.1, bf16[512,512]{1,0:T(8,128)(2,1)} %wproj_hbm.1, bf16[512,1024]{1,0:T(8,128)(2,1)} %wkv_hbm.1, ...), custom_call_target="tpu_custom_call" | custom-call | tf_op jit(solution)/shard_map/pallas_call | solution.py:447
  29.0 0.7 %copy.20 = bf16[2,6,24,512]{3,2,1,0:T(8,128)(2,1)} copy(bf16[2,6,24,512]{3,2,1,0:T(8,128)(2,1)S(1)} %bitcast.8) | data formatting | bytes 589824
  29.7 0.7 %copy.21 = bf16[2,24,1920]{2,1,0:T(8,128)(2,1)} copy(bf16[2,24,1920]{2,1,0:T(8,128)(2,1)S(1)} %bitcast.9) | data formatting | bytes 368640

commit v4 on v3

--- a/solution.py
+++ b/solution.py
@@ -107,6 +107,7 @@
     packed_ref,
     packed_halo_ref,
     attended_ref,
+    share_ref,
     mixed_ref,
     level_query_ref,
     expand_ref,
@@ -331,12 +332,54 @@
         q_inner = packed_ref[inner, pl.ds(128 * quad, 128)]
         k_inner = packed_ref[inner, pl.ds(WIDTH + 128 * quad, 128)]
         v_inner = packed_ref[inner, pl.ds(2 * WIDTH + 128 * quad, 128)]
-        out = jnp.zeros((TOKENS, 128), F32)
-        for j in range(4):
-            mine = lane128 // HEAD_DIM == j
-            weights = soft(dot_nt(jnp.where(mine, q_inner, zero), k_inner) + bias_ref[4 * quad + j])
-            out = jnp.where(mine, dot_nn(weights, v_inner), out)
+        q_heads = jnp.concatenate(
+            [jnp.where(lane128 // HEAD_DIM == j, q_inner, zero) for j in range(4)], axis=0
+        )
+        bias = bias_ref[pl.ds(4 * quad, 4)].reshape(4 * TOKENS, TOKENS)
+        heads = dot_nn(soft(dot_nt(q_heads, k_inner) + bias), v_inner)
+        out = heads[:TOKENS]
+        for j in range(1, 4):
+            part = heads[TOKENS * j : TOKENS * j + TOKENS]
+            out = jnp.where(lane128 // HEAD_DIM == j, part, out)
         attended_ref[inner, pl.ds(128 * quad, 128)] = out.astype(BF16)
+
+    lane = lax.broadcasted_iota(jnp.int32, (1, TOKENS), 1)
+    upper_key = lane - 12 * over_twelve(lane) >= 12 - offset
+    side = jnp.where(upper, 1, 0) + jnp.zeros((TOKENS, TOKENS), jnp.int32)
+    same = side == jnp.where(upper_key, 1, 0)
+    edge = pl.ds(TOKENS, TOKENS)
+
+    def by_head(rows):
+        out = rows(0)
+        for j in range(1, 4):
+            out = jnp.where(lane128 // HEAD_DIM == j, rows(j), out)
+        return out
+
+    def share(quad, keys, values, met):
+        query = packed_ref[edge, pl.ds(128 * quad, 128)]
+        q_heads = jnp.concatenate(
+            [jnp.where(lane128 // HEAD_DIM == j, query, zero) for j in range(4)], axis=0
+        )
+        bias = jnp.where(met[None], bias_ref[pl.ds(4 * quad, 4)], -1e30)
+        scores = dot_nt(q_heads, keys) + bias.reshape(4 * TOKENS, TOKENS)
+        peak = jnp.max(scores, axis=-1, keepdims=True)
+        raised = jnp.exp2(scores - peak)
+        total = jnp.sum(raised, axis=-1, keepdims=True)
+        heads = dot_nn(raised.astype(BF16), values)
+        return [
+            by_head(lambda j: value[TOKENS * j : TOKENS * j + TOKENS])
+            for value in (peak, total, heads)
+        ]
+
+    for quad in range(4):
+        found = share(
+            quad,
+            packed_ref[edge, pl.ds(WIDTH + 128 * quad, 128)],
+            packed_ref[edge, pl.ds(2 * WIDTH + 128 * quad, 128)],
+            same,
+        )
+        for i in range(3):
+            share_ref[i, :, pl.ds(128 * quad, 128)] = found[i]
 
     finish(0, ((2, 3, 1, 0),))
 
@@ -344,33 +387,21 @@
         copy.wait()
     halo = jnp.where(upper, halo_ref[1].astype(F32), halo_ref[0].astype(F32)).astype(BF16)
     packed_halo_ref[...] = dot_nn(halo, wqkv_ref[:, WIDTH:]).astype(BF16)
-    lane256 = lax.broadcasted_iota(jnp.int32, (TOKENS, 256), 1)
-    edge = pl.ds(TOKENS, TOKENS)
     for quad in range(4):
-        q_edge = packed_ref[edge, pl.ds(128 * quad, 128)].astype(F32)
-        k_edge = packed_ref[edge, pl.ds(WIDTH + 128 * quad, 128)].astype(F32)
-        v_edge = packed_ref[edge, pl.ds(2 * WIDTH + 128 * quad, 128)].astype(F32)
-        k_halo = packed_halo_ref[:, pl.ds(128 * quad, 128)].astype(F32)
-        v_halo = packed_halo_ref[:, pl.ds(WIDTH + 128 * quad, 128)].astype(F32)
-        q_both = jnp.concatenate([jnp.where(upper, q_edge, 0.0), jnp.where(upper, 0.0, q_edge)], 1)
-        k_both = jnp.concatenate(
-            [jnp.where(upper, k_edge, k_halo), jnp.where(upper, k_halo, k_edge)], 1
-        )
-        v_both = jnp.concatenate(
-            [jnp.where(upper, v_edge, v_halo), jnp.where(upper, v_halo, v_edge)], 1
-        )
-        q_both, k_both, v_both = q_both.astype(BF16), k_both.astype(BF16), v_both.astype(BF16)
-        out_upper = jnp.zeros((TOKENS, 128), F32)
-        out_lower = jnp.zeros((TOKENS, 128), F32)
-        for j in range(4):
-            mine = lane256 % 128 // HEAD_DIM == j
-            weights = soft(dot_nt(jnp.where(mine, q_both, zero), k_both) + bias_ref[4 * quad + j])
-            both = dot_nn(weights, v_both)
-            mine = lane128 // HEAD_DIM == j
-            out_upper = jnp.where(mine, both[:, :128], out_upper)
-            out_lower = jnp.where(mine, both[:, 128:], out_lower)
-        out = jnp.where(upper, out_upper, out_lower)
-        attended_ref[edge, pl.ds(128 * quad, 128)] = out.astype(BF16)
+        lanes = pl.ds(128 * quad, 128)
+        far_peak, far_total, far_out = share(
+            quad,
+            packed_halo_ref[:, lanes],
+            packed_halo_ref[:, pl.ds(WIDTH + 128 * quad, 128)],
+            jnp.logical_not(same),
+        )
+        near_peak = share_ref[0, :, lanes]
+        peak = jnp.maximum(near_peak, far_peak)
+        near_scale = jnp.exp2(near_peak - peak)
+        far_scale = jnp.exp2(far_peak - peak)
+        total = share_ref[1, :, lanes] * near_scale + far_total * far_scale
+        out = (share_ref[2, :, lanes] * near_scale + far_out * far_scale) / total
+        attended_ref[edge, lanes] = out.astype(BF16)
 
     finish(1, ((2, 3), (1, 0)))
 
@@ -476,6 +507,7 @@
             pltpu.VMEM((OWN, 3 * WIDTH), BF16),
             pltpu.VMEM((TOKENS, 2 * WIDTH), BF16),
             pltpu.VMEM((OWN, WIDTH), BF16),
+            pltpu.VMEM((3, TOKENS, WIDTH), F32),
             pltpu.VMEM((OWN, WIDTH), BF16),
             pltpu.VMEM((128, WIDTH), BF16),
             pltpu.VMEM((256, WIDTH), BF16),

time: 30.5 us -> 30.2 us (level)
    pallas_call x1, Pallas kernels: 27.7 us -> 27.4 us  [body(): pl.pallas_call(functools.partial(kernel, lon_count, lev_count), out_shape...]
where the time goes in v4:
time: 30.2 us; the launch traced here: 30.1 us
  Pallas kernels  27.4 us (91%)
  local copies, waits for them, and re-layouts  1.39 us (5%)
  between operations  1.29 us (4%)
    pallas_call x1, Pallas kernels, body(): pl.pallas_call(functools.partial(kernel, lon_count, lev_count), out_shape...  27.4 us
    unnamed x2, local copies, waits for them, and re-layouts  1.39 us

profile of v4, /device:TPU:64, one launch (start us, length us, event | category | flops | bytes accessed | tf_op | source)
XLA Modules:
  0.0 30.1 jit_solution(15990260412103489179)
XLA Ops:
  1.3 27.4 %shard_map.158 = (bf16[288,512]{1,0:T(8,128)(2,1)S(1)}, bf16[48,1920]{1,0:T(8,128)(2,1)S(1)}) custom-call(s32[1]{0:T(128)S(6)} %copy.19.offset_hbm, s32[8]{0:T(128)} %order_hbm.1, bf16[288,512]{1,0:T(8,128)(2,1)} %bitcast.10, bf16[512,1536]{1,0:T(8,128)(2,1)} %wqkv_hbm.1, bf16[512,512]{1,0:T(8,128)(2,1)} %wproj_hbm.1, bf16[512,1024]{1,0:T(8,128)(2,1)} %wkv_hbm.1, ...), custom_call_target="tpu_custom_call" | custom-call | tf_op jit(solution)/shard_map/pallas_call | solution.py:478
  28.7 0.7 %copy.20 = bf16[2,6,24,512]{3,2,1,0:T(8,128)(2,1)} copy(bf16[2,6,24,512]{3,2,1,0:T(8,128)(2,1)S(1)} %bitcast.8) | data formatting | bytes 589824
  29.4 0.7 %copy.21 = bf16[2,24,1920]{2,1,0:T(8,128)(2,1)} copy(bf16[2,24,1920]{2,1,0:T(8,128)(2,1)S(1)} %bitcast.9) | data formatting | bytes 368640

commit v5 on v4

--- a/solution.py
+++ b/solution.py
@@ -178,7 +178,7 @@
     cells = lax.broadcasted_iota(jnp.int32, (OWN, OWN), 1)
     turn = jnp.where(cells == turned_col, 1.0, 0.0).astype(BF16)
     loaded("latents")
-    turned_ref[...] = dot_nn(turn, own_ref[...]).astype(BF16)
+    turned_ref[pl.ds(TOKENS, TOKENS), :] = dot_nn(turn[TOKENS:], own_ref[...]).astype(BF16)
 
     pl.semaphore_wait(barrier, 2 + lev_count - 1)
     halo_copies = []
@@ -193,6 +193,8 @@
         )
         copy.start()
         halo_copies.append(copy)
+
+    turned_ref[pl.ds(0, TOKENS), :] = dot_nn(turn[:TOKENS], own_ref[...]).astype(BF16)
 
     lane24 = lax.broadcasted_iota(jnp.int32, (24, 128), 1)
     loaded("coords", "first", "first_offset", "second", "compact")
@@ -420,32 +422,27 @@
     base = 48 * source + 24 * slot + 4 * (lat - 6 * source)
     place = lax.broadcasted_iota(jnp.int32, (48, rows), 1) - base
     gather = jnp.concatenate([jnp.where(place == q, 1.0, 0.0) for q in range(4)], 0).astype(BF16)
-    parts = [[] for _ in range(ROW // 128)]
+    shift = TILE * offset
+    count = ROW // 128
+    source_lane = lax.broadcasted_iota(jnp.int32, (256, WIDTH), 0)
+    step_lane = lax.broadcasted_iota(jnp.int32, (256, WIDTH), 1) - source_lane - (shift & 127)
+    step_lane = jnp.where(source_lane < 3 * TILE, step_lane, -1)
+    firsts = [[960 * half + 240 * q for q in range(4)] for half in range(2)]
+    slides = [
+        [jnp.where(step_lane == first % 128, 1.0, 0.0).astype(BF16) for first in row]
+        for row in firsts
+    ]
+    tiles = [None] * count
     for half in range(2):
         for copy in tile_copies[half]:
             copy.wait()
-        sorted_rows = dot_nn(gather, receive_ref[half].reshape(rows, 256))
+        sorted_rows = dot_nn(gather, receive_ref[half].reshape(rows, 256)).astype(BF16)
         for q in range(4):
-            for c in range(2):
-                part = sorted_rows[48 * q : 48 * q + 48, 128 * c : 128 * c + 128]
-                first = 960 * half + 240 * q + 128 * c
-                if first % 128:
-                    part = pltpu.roll(part, first % 128, 1)
-                last = first + (127 if c == 0 else 111)
-                for k in range(first // 128, last // 128 + 1):
-                    parts[k].append((first - 128 * k, part))
-    shift = TILE * offset
-    count = ROW // 128
-    tiles = [piece(part).astype(BF16) for part in parts]
-    pairs = jnp.concatenate(
-        [jnp.concatenate([tiles[k - 1], tiles[k]], axis=1) for k in range(count)], axis=0
-    )
-    slide = lax.broadcasted_iota(jnp.int32, (256, 128), 0) - lax.broadcasted_iota(
-        jnp.int32, (256, 128), 1
-    )
-    slide = jnp.where(slide == 128 - (shift & 127), 1.0, 0.0).astype(BF16)
-    turned_lanes = dot_nn(pairs, slide)
-    tiles = [turned_lanes[48 * k : 48 * k + 48] for k in range(count)]
+            slid = dot_nn(sorted_rows[48 * q : 48 * q + 48], slides[half][q])
+            for t in range(4):
+                k = (firsts[half][q] // 128 + t) % count
+                part = slid[:, 128 * t : 128 * t + 128]
+                tiles[k] = part if tiles[k] is None else tiles[k] + part
     whole = jnp.zeros((48, 128), jnp.int32) + lax.shift_right_logical(shift, 7)
     for bit in (1, 2, 4):
         chosen = whole & bit != 0

time: 30.2 us -> 30.4 us (level)
  no operation moved by 1% of the time
where the time goes in v5:
time: 30.4 us; the launch traced here: 30.3 us
  Pallas kernels  27.6 us (91%)
  local copies, waits for them, and re-layouts  1.39 us (5%)
  between operations  1.29 us (4%)
    pallas_call x1, Pallas kernels, body(): pl.pallas_call(functools.partial(kernel, lon_count, lev_count), out_shape...  27.6 us
    unnamed x2, local copies, waits for them, and re-layouts  1.39 us

profile of v5, /device:TPU:64, one launch (start us, length us, event | category | flops | bytes accessed | tf_op | source)
XLA Modules:
  0.0 30.3 jit_solution(4870523017237626476)
XLA Ops:
  1.3 27.6 %shard_map.158 = (bf16[288,512]{1,0:T(8,128)(2,1)S(1)}, bf16[48,1920]{1,0:T(8,128)(2,1)S(1)}) custom-call(s32[1]{0:T(128)S(6)} %copy.19.offset_hbm, s32[8]{0:T(128)} %order_hbm.1, bf16[288,512]{1,0:T(8,128)(2,1)} %bitcast.10, bf16[512,1536]{1,0:T(8,128)(2,1)} %wqkv_hbm.1, bf16[512,512]{1,0:T(8,128)(2,1)} %wproj_hbm.1, bf16[512,1024]{1,0:T(8,128)(2,1)} %wkv_hbm.1, ...), custom_call_target="tpu_custom_call" | custom-call | tf_op jit(solution)/shard_map/pallas_call | solution.py:475
  28.9 0.7 %copy.20 = bf16[2,6,24,512]{3,2,1,0:T(8,128)(2,1)} copy(bf16[2,6,24,512]{3,2,1,0:T(8,128)(2,1)S(1)} %bitcast.8) | data formatting | bytes 589824
  29.6 0.7 %copy.21 = bf16[2,24,1920]{2,1,0:T(8,128)(2,1)} copy(bf16[2,24,1920]{2,1,0:T(8,128)(2,1)S(1)} %bitcast.9) | data formatting | bytes 368640
